TPU v7x, 256 devices: a whole 4x4x8 slice. The times are simulated.
256 devices in a mesh: rows: 64 (over y, z, core), grp: 4 (over x).
Axes of the slice: x: 4, y: 4, z: 8, core: 2. Of those that a mesh axis runs over, the one named last changes fastest.
Arguments:
- sensitivity: bfloat16 [4, 1048576, 256], P('grp', 'rows')
- block_moves: int32 [4, 64, 4], P('grp', 'rows'), may hold values from 0 to 32, as said below
- shape_modes: bfloat16 [4, 524288, 128], P('grp', 'rows'), may hold values from -6 to 6
Outputs:
- factor: float32 [256, 256], replicated
- projection: float32 [128, 256], replicated
Inputs may be any that keep to these rules, and one draw needn't show every extreme that they name: block_moves[g, d] = (h, t, p, n): device d holds 64 + h + t - p - n valid blocks in its first slots, in row order; its first h go to device d - 1 and its last t to device d + 1; p is the t of device d - 1 and n the h of device d + 1, both 0 where that device does not exist; of the t of device d and the h of device d + 1 at most one is nonzero; p + n <= 64.
All inputs are finite; a program needn't handle non-finite values.
Results may differ from a plain program's by a relative error of at most 0.00455.
The roundings to bfloat16 on the way count: a program that leaves them out, or rounds other values in their place, can miss the bound.
Values may be sent and summed in bfloat16 or wider, within the bound.
No kernel may reach another device: no remote copies, remote signals or barrier semaphores. Data moves between devices by JAX's collectives and lax.ppermute only.
A program may use at most 128 MiB of HBM per device.

v0:
```python
import jax
import jax.numpy as jnp
from jax import lax
from jax.sharding import PartitionSpec as P

BLOCK = 128


def passed_along(block, axis, distance):
    devices = range(lax.axis_size(axis))
    route = [(i - distance, i) for i in devices if i - distance in devices]
    return lax.ppermute(block, axis, route)


def upper_factor(gram):
    size = gram.shape[0]
    columns = jnp.arange(size, dtype=jnp.int32)

    def step(k, carry):
        rest, factor = carry
        row = lax.dynamic_index_in_dim(rest, k, 0, keepdims=False)
        pivot = lax.dynamic_index_in_dim(row, k, 0, keepdims=False)
        row = jnp.where(columns >= k, row / jnp.sqrt(pivot), jnp.zeros_like(row))
        rest = rest - row[:, None] * row[None, :]
        factor = lax.dynamic_update_index_in_dim(factor, row, k, 0)
        return (rest, factor)

    result = lax.fori_loop(0, size, step, (gram, jnp.zeros_like(gram)))
    return result[1]


def upper_inverse(factor):
    size = factor.shape[0]
    columns = jnp.arange(size, dtype=jnp.int32)

    def step(i, result):
        k = size - 1 - i
        row = lax.dynamic_index_in_dim(factor, k, 0, keepdims=False)
        diag = lax.dynamic_index_in_dim(row, k, 0, keepdims=False)
        beyond = jnp.where(columns > k, row, jnp.zeros_like(row))
        unit = jnp.where(columns == k, jnp.ones_like(row), jnp.zeros_like(row))
        fresh = (unit - jnp.dot(beyond, result, precision=lax.Precision.HIGHEST)) / diag
        return lax.dynamic_update_index_in_dim(result, fresh, k, 0)

    return lax.fori_loop(0, size, step, jnp.zeros_like(factor))


def local_gram(panel_rows):
    return lax.dot_general(
        panel_rows, panel_rows, (((0,), (0,)), ((), ())), preferred_element_type=jnp.float32
    )


def whole_factor(gram_local):
    total = lax.psum(gram_local, ("rows", "grp"))
    return upper_factor(total)


def rows_to_owner(blocks, head_count, prev_tail, own_count, drift_count, block_total):
    slot_count = blocks.shape[0]
    pick = jnp.clip(
        head_count + own_count + jnp.arange(drift_count, dtype=jnp.int32), 0, slot_count - 1
    )
    outgoing_tail = jnp.take(blocks, pick, axis=0)
    outgoing_head = blocks[:drift_count]
    from_prev = passed_along(outgoing_tail, "rows", 1)
    from_next = passed_along(outgoing_head, "rows", -1)
    pooled = jnp.concatenate([from_prev, blocks, from_next], axis=0)
    target = jnp.arange(block_total, dtype=jnp.int32)
    index = jnp.where(
        target < prev_tail,
        target,
        jnp.where(
            target < prev_tail + own_count,
            drift_count + head_count + target - prev_tail,
            drift_count + slot_count + target - prev_tail - own_count,
        ),
    )
    balanced = jnp.take(pooled, jnp.clip(index, 0, pooled.shape[0] - 1), axis=0)
    return balanced.reshape(-1, blocks.shape[2])


def body(sensitivity, block_moves, shape_modes):
    members = sensitivity.shape[2]
    blocks = sensitivity[0].reshape(-1, BLOCK, members)
    mode_rows = shape_modes[0]
    mode_count = mode_rows.shape[1]
    mode_blocks = mode_rows.reshape(-1, BLOCK, mode_count)
    block_total = mode_blocks.shape[0]
    drift_count = block_total // 2
    head_count = block_moves[0, 0, 0]
    prev_tail = block_moves[0, 0, 2]
    next_head = block_moves[0, 0, 3]
    own_count = block_total - prev_tail - next_head
    panel_rows = rows_to_owner(blocks, head_count, prev_tail, own_count, drift_count, block_total)
    factor = whole_factor(local_gram(panel_rows))
    inverse = upper_inverse(factor).astype(jnp.bfloat16)
    ortho_rows = jnp.dot(panel_rows, inverse, preferred_element_type=jnp.float32).astype(
        jnp.bfloat16
    )
    partial_sum = lax.dot_general(
        mode_rows, ortho_rows, (((0,), (0,)), ((), ())), preferred_element_type=jnp.float32
    )
    projection = lax.psum(partial_sum, ("rows", "grp"))
    return (factor, projection)


def solution(mesh):
    return jax.shard_map(
        body,
        mesh=mesh,
        in_specs=(P("grp", "rows", None), P("grp", "rows", None), P("grp", "rows", None)),
        out_specs=(P(), P()),
        check_vma=False,
    )
```

profile of v0, /device:TPU:1, one launch (start us, length us, event | category | flops | bytes accessed | tf_op | source)
XLA Modules:
  0.0 2138.2 jit_solution(8422187432427972262)
XLA Ops:
  10.6 5.4 gather_fusion
  16.0 3.1 broadcast_select_fusion.1
  19.1 4.9 collective-permute-start
  24.1 3.1 slice.18
  27.1 2.8 collective-permute-start.1
  32.6 14.7 collective-permute-done
  47.3 7.5 collective-permute-done.1
  54.8 13.3 pad_maximum_fusion
  68.1 7.3 gather_fusion.1
  75.4 6.2 fusion.12
  81.6 5.3 bitcast_select_fusion
  86.9 246.1 %all-reduce.3.cloned.1.call-done = f32[256,256]{1,0:T(8,128)} async-done(((f32[256,256]{1,0:T(8,128)}), f32[256,256]{1,0:T(8,128)}) %all-reduce.3.cloned.1.call-update) | async-done | bytes 262160 | tf_op jit(solution)/shard_map/psum | solution.py:55
  333.0 1148.3 %while.37 = (s32[]{:T(128)}, f32[256,256]{1,0:T(8,128)}, f32[256,256]{1,0:T(8,128)S(1)}, s32[]{:T(128)}, s32[]{:T(128)}, /*index=5*/s32[]{:T(128)}) while((s32[]{:T(128)}, f32[256,256]{1,0:T(8,128)}, f32[256,256]{1,0:T(8,128)S(1)}, s32[]{:T(128)}, s32[]{:T(128)}, /*index=5*/s32[]{:T(128)}) %tuple.93), condition=%wide.region_2.3_spmd.clone, body=%wide.region_1.2_spmd.clone.sunk | while | flops 132355 | bytes 534141 | solution.py:28
  335.7 1.8 multiply_subtract_fusion.2
  340.2 1.8 multiply_subtract_fusion.2
  344.6 1.8 multiply_subtract_fusion.2
  349.1 1.8 multiply_subtract_fusion.2
  353.6 1.8 multiply_subtract_fusion.2
  371.5 1.8 multiply_subtract_fusion.2
  385.0 1.8 multiply_subtract_fusion.2
  393.9 1.8 multiply_subtract_fusion.2
  398.4 1.8 multiply_subtract_fusion.2
  407.4 1.8 multiply_subtract_fusion.2
  411.9 1.8 multiply_subtract_fusion.2
  420.9 1.8 multiply_subtract_fusion.2
  425.4 1.8 multiply_subtract_fusion.2
  438.8 1.8 multiply_subtract_fusion.2
  447.8 1.8 multiply_subtract_fusion.2
  452.3 1.8 multiply_subtract_fusion.2
  461.2 1.8 multiply_subtract_fusion.2
  470.2 1.8 multiply_subtract_fusion.2
  479.2 1.8 multiply_subtract_fusion.2
  483.7 1.8 multiply_subtract_fusion.2
  501.6 1.8 multiply_subtract_fusion.2
  506.1 1.8 multiply_subtract_fusion.2
  515.0 1.8 multiply_subtract_fusion.2
  519.5 1.8 multiply_subtract_fusion.2
  524.0 1.8 multiply_subtract_fusion.2
  528.5 1.8 multiply_subtract_fusion.2
  533.0 1.8 multiply_subtract_fusion.2
  550.9 1.8 multiply_subtract_fusion.2
  555.4 1.8 multiply_subtract_fusion.2
  568.8 1.8 multiply_subtract_fusion.2
  573.3 1.8 multiply_subtract_fusion.2
  649.6 1.8 multiply_subtract_fusion.2
  1481.3 401.8 %while.38 = (s32[]{:T(128)}, f32[256,256]{1,0:T(8,128)S(1)}, f32[256,256]{1,0:T(8,128)S(1)}, s32[]{:T(128)}, s32[]{:T(128)}, /*index=5*/s32[]{:T(128)}, s32[]{:T(128)}) while((s32[]{:T(128)}, f32[256,256]{1,0:T(8,128)S(1)}, f32[256,256]{1,0:T(8,128)S(1)}, s32[]{:T(128)}, s32[]{:T(128)}, /*index=5*/s32[]{:T(128)}, ...), condition=%wide.region_4.5_spmd.clone.clone, body=%wide.region_3.4_spmd.clone.clone.sunk | while | flops 787975 | bytes 272555 | solution.py:45
  1883.1 5.5 fusion.15
  1888.6 241.1 %all-reduce.5.cloned.1.call-done = f32[128,256]{0,1:T(8,128)} async-done(((f32[128,256]{0,1:T(8,128)}), f32[128,256]{0,1:T(8,128)}) %all-reduce.5.cloned.1.call-update) | async-done | bytes 131088 | tf_op jit(solution)/shard_map/psum | solution.py:104
  (3059 shorter events, 1301.6 us)
Async XLA Ops:
  7.2 1875.9 %copy-start = (bf16[1,8192,128]{2,1,0:T(8,128)(2,1)S(1)}, bf16[1,8192,128]{2,1,0:T(8,128)(2,1)}, u32[]{:S(2)}) copy-start(bf16[1,8192,128]{2,1,0:T(8,128)(2,1)} %param.9) | copy-start | bytes 6291460
  7.2 325.8 %all-reduce.3.cloned.1.call-start = ((), (), s32[]{:S(2)}) async-start(), calls=%async_computation | async-start | bytes 524288 | tf_op jit(solution)/shard_map/psum | solution.py:55
  19.1 28.2 %collective-permute-start = (bf16[32,128,256]{2,1,0:T(8,128)(2,1)}, bf16[32,128,256]{2,1,0:T(8,128)(2,1)}, u32[]{:S(2)}, u32[]{:S(2)}) collective-permute-start(bf16[32,128,256]{2,1,0:T(8,128)(2,1)} %broadcast_select_fusion.1), channel_id=1, source_target_pairs={{0,4},{4,8},{8,12},{12,16},{16,20},{20,24},{24,28},{28,32},{32,36}... | collective-permute-start | bytes 6291464 | tf_op jit(solution)/shard_map/ppermute | solution.py:12
  27.1 27.7 %collective-permute-start.1 = (bf16[32,128,256]{2,1,0:T(8,128)(2,1)}, bf16[32,128,256]{2,1,0:T(8,128)(2,1)}, u32[]{:S(2)}, u32[]{:S(2)}) collective-permute-start(bf16[32,128,256]{2,1,0:T(8,128)(2,1)} %bitcast.5), channel_id=1, source_target_pairs={{4,0},{8,4},{12,8},{16,12},{20,16},{24,20},{28,24},{32,28},{36,32}... | collective-permute-start | bytes 6291464 | tf_op jit(solution)/shard_map/ppermute | solution.py:12
  81.6 2048.1 %all-reduce.5.cloned.1.call-start = ((), (), s32[]{:S(2)}) async-start(), calls=%async_computation.1 | async-start | bytes 262144 | tf_op jit(solution)/shard_map/psum | solution.py:104
  1883.1 5.5 copy-start.1
Sparse Core Ops, SparseCore 0:
  81.7 251.1 all-reduce.2
  1888.7 240.9 all-reduce.4
where the time goes:
time: 2170 us; the launch traced here: 2140 us
  other arithmetic  824 us (38%)
  local copies, waits for them, and re-layouts  524 us (24%)
  waiting for transfers between devices  509 us (23%)
  loops' own time  197 us (9%)
  matrix products  59 us (3%)
    sub x256, other arithmetic, step(): rest = rest - row[:, None] * row[None, :]  449 us
    dynamic_slice x256, local copies, waits for them, and re-layouts, step(): pivot = lax.dynamic_index_in_dim(row, k, 0, keepdims=False)  324 us
    psum x1, waiting for transfers between devices, whole_factor(): total = lax.psum(gram_local, ('rows', 'grp'))  246 us
    psum x1, waiting for transfers between devices, body(): projection = lax.psum(partial_sum, ('rows', 'grp'))  241 us
    another operation x1, loops' own time, upper_factor(): result = lax.fori_loop(0, size, step, (gram, jnp.zeros_like(gram)))  184 us
    select_n x512, other arithmetic, step(): row = jnp.where(columns >= k, row / jnp.sqrt(pivot), jnp.zeros_like(row))  183 us
    div x256, other arithmetic, step(): (unit - jnp.dot(beyond, result, precision=lax.Precision.HIGHEST)) / diag  166 us
    dynamic_slice x256, local copies, waits for them, and re-layouts, step(): diag = lax.dynamic_index_in_dim(row, k, 0, keepdims=False)  161 us
  transfers between devices with their start and end apart: 4, of which 4 were waited for; matrix products, arithmetic and copies ran while one was open for 0% of the time, Pallas kernels for 0%

commit v1 on v0

v1 whole, which is shorter than its diff:
```python
import jax
import jax.numpy as jnp
from jax import lax
from jax.experimental import pallas as pl
from jax.experimental.pallas import tpu as pltpu
from jax.sharding import Mesh, PartitionSpec as P

BLOCK = 128
LANES = 128
MEMBERS = 256
MODES = 128
CHUNK = 8
CHUNK_ROWS = CHUNK * BLOCK
TILE = 8
STACK = 768


def transposed_product(a, b):
    return lax.dot_general(a, b, (((0,), (0,)), ((), ())), preferred_element_type=jnp.float32)


def kept_rows(values, first, start, stop):
    row = first + lax.broadcasted_iota(jnp.int32, values.shape, 0)
    keep = (row >= start) & (row < stop)
    return jnp.where(keep, values, jnp.zeros_like(values))


def own_rows_kernel(moves, panel, modes, out, panel_v, modes_v, gram, cross, panel_sem, modes_sem):
    head, tail, prev, following = moves[0], moves[1], moves[2], moves[3]
    block_total = modes.shape[0] // BLOCK
    lead = block_total // 2
    own = block_total - prev - following
    valid = head + own + tail
    steps = jnp.maximum(lax.div(valid + (CHUNK - 1), CHUNK), 2)

    def panel_copy(i):
        rows = pl.ds(pl.multiple_of(i * CHUNK_ROWS, CHUNK_ROWS), CHUNK_ROWS)
        return pltpu.make_async_copy(panel.at[rows], panel_v.at[rows], panel_sem.at[i])

    shift = pl.multiple_of((lead + head - prev) * BLOCK, BLOCK)
    modes_copy = pltpu.make_async_copy(
        modes, modes_v.at[pl.ds(shift, modes.shape[0])], modes_sem
    )
    for i in range(2):
        panel_copy(i).start()
    modes_copy.start()

    def launch(i, carry):
        panel_copy(i).start()
        return carry

    lax.fori_loop(2, steps, launch, 0)
    gram[...] = jnp.zeros_like(gram)
    cross[...] = jnp.zeros_like(cross)

    def step(i, carry):
        first = i * CHUNK_ROWS
        panel_copy(i).wait()

        @pl.when(i == 0)
        def _():
            modes_copy.wait()

        rows = pl.ds(pl.multiple_of(first, CHUNK_ROWS), CHUNK_ROWS)
        values = panel_v[rows, :]
        gram[...] += transposed_product(kept_rows(values, first, 0, valid * BLOCK), values)
        beside = pl.ds(pl.multiple_of(first + lead * BLOCK, CHUNK_ROWS), CHUNK_ROWS)
        mode_values = kept_rows(modes_v[beside, :], first, head * BLOCK, (head + own) * BLOCK)
        cross[...] += transposed_product(mode_values, values)
        return carry

    lax.fori_loop(0, steps, step, 0)
    for i in range(2):
        for j in range(2):
            start = (2 * i + j) * LANES
            out[start : start + LANES, :] = gram[i * LANES : (i + 1) * LANES, j * LANES : (j + 1) * LANES]
        out[(4 + i) * LANES : (5 + i) * LANES, :] = cross[:, i * LANES : (i + 1) * LANES]


def edge_rows_kernel(
    moves, panel, from_prev, from_next, before, out, head_v, tail_v, prev_v, next_v, cross, sems
):
    head, tail, prev, following = moves[0], moves[1], moves[2], moves[3]
    edge_rows = from_prev.shape[0]
    lead = edge_rows // BLOCK
    own = 2 * lead - prev - following
    tail_start = pl.multiple_of((head + own) * BLOCK, BLOCK)
    shift = pl.multiple_of(head * BLOCK, BLOCK)
    copies = [
        pltpu.make_async_copy(panel.at[pl.ds(0, edge_rows)], head_v, sems.at[0]),
        pltpu.make_async_copy(from_prev, prev_v.at[pl.ds(shift, edge_rows)], sems.at[1]),
        pltpu.make_async_copy(panel.at[pl.ds(tail_start, edge_rows)], tail_v, sems.at[2]),
        pltpu.make_async_copy(from_next, next_v, sems.at[3]),
    ]
    for copy in copies:
        copy.start()
    cross[...] = jnp.zeros_like(cross)
    for copy in copies:
        copy.wait()

    def head_step(i, carry):
        first = i * CHUNK_ROWS
        rows = pl.ds(pl.multiple_of(first, CHUNK_ROWS), CHUNK_ROWS)
        beside = pl.ds(pl.multiple_of(first + edge_rows, CHUNK_ROWS), CHUNK_ROWS)
        mode_values = kept_rows(prev_v[beside, :], first, 0, head * BLOCK)
        cross[...] += transposed_product(mode_values, head_v[rows, :])
        return carry

    def tail_step(i, carry):
        first = i * CHUNK_ROWS
        rows = pl.ds(pl.multiple_of(first, CHUNK_ROWS), CHUNK_ROWS)
        mode_values = kept_rows(next_v[rows, :], first, 0, tail * BLOCK)
        cross[...] += transposed_product(mode_values, tail_v[rows, :])
        return carry

    lax.fori_loop(0, lax.div(head + (CHUNK - 1), CHUNK), head_step, 0)
    lax.fori_loop(0, lax.div(tail + (CHUNK - 1), CHUNK), tail_step, 0)
    out[: 4 * LANES, :] = before[: 4 * LANES, :]
    for i in range(2):
        rows = slice((4 + i) * LANES, (5 + i) * LANES)
        out[rows, :] = before[rows, :] + cross[:, i * LANES : (i + 1) * LANES]


def own_rows(moves, panel, modes):
    slots = panel.shape[0] // BLOCK
    spare = modes.shape[0] // 2
    return pl.pallas_call(
        own_rows_kernel,
        out_shape=jax.ShapeDtypeStruct((STACK, LANES), jnp.float32),
        in_specs=[
            pl.BlockSpec(memory_space=pltpu.SMEM),
            pl.BlockSpec(memory_space=pl.ANY),
            pl.BlockSpec(memory_space=pl.ANY),
        ],
        out_specs=pl.BlockSpec(memory_space=pltpu.VMEM),
        scratch_shapes=[
            pltpu.VMEM(panel.shape, panel.dtype),
            pltpu.VMEM((panel.shape[0] + spare, MODES), modes.dtype),
            pltpu.VMEM((MEMBERS, MEMBERS), jnp.float32),
            pltpu.VMEM((MODES, MEMBERS), jnp.float32),
            pltpu.SemaphoreType.DMA((slots // CHUNK,)),
            pltpu.SemaphoreType.DMA,
        ],
        compiler_params=pltpu.CompilerParams(vmem_limit_bytes=32 * 1024 * 1024),
        cost_estimate=pl.CostEstimate(
            flops=2 * 12288 * 384 * 256, bytes_accessed=10 * 1024 * 1024, transcendentals=0
        ),
        name="own_rows",
    )(moves, panel, modes)


def edge_rows(moves, panel, from_prev, from_next, before):
    rows = from_prev.shape[0]
    return pl.pallas_call(
        edge_rows_kernel,
        out_shape=jax.ShapeDtypeStruct((STACK, LANES), jnp.float32),
        in_specs=[
            pl.BlockSpec(memory_space=pltpu.SMEM),
            pl.BlockSpec(memory_space=pl.ANY),
            pl.BlockSpec(memory_space=pl.ANY),
            pl.BlockSpec(memory_space=pl.ANY),
            pl.BlockSpec(memory_space=pltpu.VMEM),
        ],
        out_specs=pl.BlockSpec(memory_space=pltpu.VMEM),
        scratch_shapes=[
            pltpu.VMEM((rows, MEMBERS), panel.dtype),
            pltpu.VMEM((rows, MEMBERS), panel.dtype),
            pltpu.VMEM((2 * rows, MODES), from_prev.dtype),
            pltpu.VMEM((rows, MODES), from_prev.dtype),
            pltpu.VMEM((MODES, MEMBERS), jnp.float32),
            pltpu.SemaphoreType.DMA((4,)),
        ],
        compiler_params=pltpu.CompilerParams(vmem_limit_bytes=32 * 1024 * 1024),
        cost_estimate=pl.CostEstimate(
            flops=2 * 4096 * 128 * 256, bytes_accessed=6 * 1024 * 1024, transcendentals=0
        ),
        name="edge_rows",
    )(moves, panel, from_prev, from_next, before)


def projected(product, inverse_t):
    high = product.astype(jnp.bfloat16)
    rest = product - high.astype(jnp.float32)
    middle = rest.astype(jnp.bfloat16)
    low = (rest - middle.astype(jnp.float32)).astype(jnp.bfloat16)

    def part(values):
        return lax.dot_general(
            values, inverse_t, (((1,), (1,)), ((), ())), preferred_element_type=jnp.float32
        )

    return part(low) + part(middle) + part(high)


def factor_kernel(core, mine, other, factor, projection, work, packed, cross):
    half = mine.shape[0]

    def place(lower, upper):
        for index in range(2 * half // LANES):
            source = lower if index * LANES < half else upper
            start = index * LANES % half
            square = source[start : start + LANES, :]
            columns = slice(index % 2 * LANES, (index % 2 + 1) * LANES)
            if index < 4:
                work[index // 2 * LANES : (index // 2 + 1) * LANES, columns] = square
            else:
                cross[:, columns] = square

    @pl.when(core[0] == 0)
    def _():
        place(mine, other)

    @pl.when(core[0] != 0)
    def _():
        place(other, mine)

    size = MEMBERS
    lanes = lax.broadcasted_iota(jnp.int32, (TILE, size), 1)
    subs = lax.broadcasted_iota(jnp.int32, (TILE, size), 0)
    near = lax.broadcasted_iota(jnp.int32, (TILE, LANES), 0)
    groups = size // TILE

    def wide(values):
        return jnp.concatenate([values, values], axis=1)

    for group in range(groups):
        base = group * TILE
        panel = work[base : base + TILE, :]
        columns = [
            jnp.broadcast_to(panel[:, base + r : base + r + 1], (TILE, LANES)) for r in range(TILE)
        ]
        for r in range(TILE):
            column = columns[r]
            pivot = jnp.broadcast_to(column[r : r + 1, :], (TILE, LANES))
            recip = 1.0 / pivot
            scale = lax.rsqrt(pivot)
            panel = jnp.where(lanes == base + r, jnp.where(subs == r, 1.0, 0.0), panel)
            row = jnp.broadcast_to(panel[r : r + 1, :], (TILE, size))
            packed[base + r : base + r + 1, :] = (row * wide(scale))[0:1]
            solved = row * wide(recip)
            panel = jnp.where(subs == r, solved, panel - wide(column) * solved)
            for s in range(r + 1, TILE):
                entry = jnp.broadcast_to(columns[s][r : r + 1, :], (TILE, LANES)) * recip
                columns[s] = jnp.where(near == r, entry, columns[s] - column * entry)
        inside = (lanes >= base) & (lanes < base + TILE)
        solved_rows = [jnp.broadcast_to(panel[q : q + 1, :], (TILE, size)) for q in range(TILE)]
        for i in range(group + 1, groups):
            rows = slice(i * TILE, (i + 1) * TILE)
            old = work[rows, :]
            fresh = jnp.where(inside, 0.0, old)
            for q in range(TILE):
                coefficient = jnp.broadcast_to(old[:, base + q : base + q + 1], (TILE, size))
                fresh = fresh - coefficient * solved_rows[q]
            work[rows, :] = fresh

    row = lax.broadcasted_iota(jnp.int32, (size, size), 0)
    column = lax.broadcasted_iota(jnp.int32, (size, size), 1)
    result = packed[...]
    factor[...] = jnp.where(
        column > row, result, jnp.where(column == row, 1.0 / result, jnp.zeros_like(result))
    )
    inverse_t = jnp.where(column <= row, result, jnp.zeros_like(result)).astype(jnp.bfloat16)
    projection[...] = projected(cross[...], inverse_t)


def factor_and_projection(core, mine, other):
    vmem = pl.BlockSpec(memory_space=pltpu.VMEM)
    return pl.pallas_call(
        factor_kernel,
        out_shape=(
            jax.ShapeDtypeStruct((MEMBERS, MEMBERS), jnp.float32),
            jax.ShapeDtypeStruct((MODES, MEMBERS), jnp.float32),
        ),
        in_specs=[pl.BlockSpec(memory_space=pltpu.SMEM), vmem, vmem],
        out_specs=(vmem, vmem),
        scratch_shapes=[
            pltpu.VMEM((MEMBERS, MEMBERS), jnp.float32),
            pltpu.VMEM((MEMBERS, MEMBERS), jnp.float32),
            pltpu.VMEM((MODES, MEMBERS), jnp.float32),
        ],
        name="factor_and_projection",
    )(core, mine, other)


def to_all(values, axes):
    count = lax.axis_size(axes)
    copies = jnp.broadcast_to(values[None], (count,) + values.shape)
    return lax.all_to_all(copies, axes, 0, 0)


def swapped(values):
    return lax.ppermute(values, "c", [(0, 1), (1, 0)])


def summed_half(stack):
    core = lax.axis_index("c")
    half = stack.shape[0] // 2
    keep = lax.dynamic_slice_in_dim(stack, core * half, half, 0)
    give = lax.dynamic_slice_in_dim(stack, (1 - core) * half, half, 0)
    share = keep + swapped(give)
    count = lax.axis_size(("y", "g"))
    pieces = share.reshape(count, half // count, LANES)
    piece = lax.all_to_all(pieces, ("y", "g"), 0, 0).sum(0)
    piece = to_all(piece, "z").sum(0)
    return to_all(piece, ("y", "g")).reshape(half, LANES)


def body(sensitivity, block_moves, shape_modes):
    panel = sensitivity[0]
    modes = shape_modes[0]
    moves = block_moves[0, 0]
    edge = modes.shape[0] // 2
    chain = ("y", "z", "c")
    count = lax.axis_size(chain)
    from_next = lax.ppermute(modes[:edge], chain, [(i + 1, i) for i in range(count - 1)])
    from_prev = lax.ppermute(modes[edge:], chain, [(i, i + 1) for i in range(count - 1)])
    stack = own_rows(moves, panel, modes)
    stack = edge_rows(moves, panel, from_prev, from_next, stack)
    mine = summed_half(stack)
    other = swapped(mine)
    core = lax.axis_index("c").astype(jnp.int32).reshape(1)
    return factor_and_projection(core, mine, other)


def solution(mesh):
    split = Mesh(mesh.devices.reshape(4, 8, 2, 4), ("y", "z", "c", "g"))
    spec = P("g", ("y", "z", "c"), None)
    return jax.shard_map(
        body, mesh=split, in_specs=(spec, spec, spec), out_specs=(P(), P()), check_vma=False
    )
```

time: 2170 us -> 89.4 us (0.04); the launches traced: 2140 us -> 89.2 us
  other arithmetic: 824 us -> 0.06 us
  local copies, waits for them, and re-layouts: 524 us -> 7.26 us
  waiting for transfers between devices: 509 us -> 7.24 us
  loops' own time: 197 us -> 0 us
  matrix products: 59 us -> 0 us
  blocking collectives: 0 us -> 40.5 us
  Pallas kernels: 0 us -> 22.3 us
    dynamic_slice x768 -> x1, local copies, waits for them, and re-layouts: 487 us -> 0.02 us  [summed_half(): give = lax.dynamic_slice_in_dim(stack, (1 - core) * half, half, 0)]
    psum x2 -> x0, waiting for transfers between devices: 487 us -> none  [the longest x1 246 us: whole_factor(): total = lax.psum(gram_local, ('rows', 'grp'))]
    sub x256 -> x0, other arithmetic: 449 us -> none  [step(): rest = rest - row[:, None] * row[None, :]]
    another operation x2 -> x0, loops' own time: 197 us -> none  [the longest x1 184 us: upper_factor(): result = lax.fori_loop(0, size, step, (gram, jnp.zeros_like(gram)))]
    select_n x772 -> x0, other arithmetic: 194 us -> none  [the longest x512 183 us: step(): row = jnp.where(columns >= k, row / jnp.sqrt(pivot), jnp.zeros_like(row))]
    div x256 -> x0, other arithmetic: 166 us -> none  [step(): (unit - jnp.dot(beyond, result, precision=lax.Precision.HIGHEST)) / diag]
    dot_general x258 -> x0, matrix products: 59 us -> none  [the longest x256 47.3 us: step(): jnp.dot(beyond, result, precision=lax.Precision.HIGHEST)]
    all_to_all x0 -> x3, blocking collectives: none -> 40.5 us  [the longest x2 24.9 us: to_all(): return lax.all_to_all(copies, axes, 0, 0)]
  transfers between devices with their start and end apart: 4 -> 4, of which waited for: 4 -> 4; matrix products, arithmetic and copies ran while one was open for 0% -> 0% of each run, Pallas kernels for 0% -> 7%
where the time goes in v1:
time: 89.4 us; the launch traced here: 89.2 us
  blocking collectives  40.5 us (45%)
  Pallas kernels  22.3 us (25%)
  starting transfers between devices  11.2 us (13%)
  local copies, waits for them, and re-layouts  7.26 us (8%)
  waiting for transfers between devices  7.24 us (8%)
    all_to_all x2, blocking collectives, to_all(): return lax.all_to_all(copies, axes, 0, 0)  24.9 us
    all_to_all x1, blocking collectives, summed_half(): piece = lax.all_to_all(pieces, ('y', 'g'), 0, 0).sum(0)  15.6 us
    pallas_call x1, Pallas kernels, factor_and_projection(): pl.pallas_call(factor_kernel, out_shape=(jax.ShapeDtypeStruct((MEMBERS, M...  12.3 us
    pallas_call x1, Pallas kernels, own_rows(): pl.pallas_call(own_rows_kernel, out_shape=jax.ShapeDtypeStruct((STACK, LA...  6.34 us
    ppermute x1, starting transfers between devices, body(): lax.ppermute(modes[edge:], chain, [(i, i + 1) for i in range(count - 1)])  4.92 us
    ppermute x1, waiting for transfers between devices, body(): lax.ppermute(modes[:edge], chain, [(i + 1, i) for i in range(count - 1)])  4.4 us
    ppermute x2, starting transfers between devices, swapped(): return lax.ppermute(values, 'c', [(0, 1), (1, 0)])  4.34 us
    unnamed x10, local copies, waits for them, and re-layouts  4.06 us
  transfers between devices with their start and end apart: 4, of which 4 were waited for; matrix products, arithmetic and copies ran while one was open for 0% of the time, Pallas kernels for 7%

profile of v1, /device:TPU:1, one launch (start us, length us, event | category | flops | bytes accessed | tf_op | source)
XLA Modules:
  0.0 89.2 jit_solution(5942710579037340894)
XLA Ops:
  0.6 0.0 copy-start.1
  0.6 0.0 copy-start.2
  0.6 3.2 %slice_bitcast_fusion = (bf16[4096,128]{1,0:T(8,128)(2,1)}, bf16[4096,128]{1,0:T(8,128)(2,1)}) fusion(bf16[1,8192,128]{2,1,0:T(8,128)(2,1)} %param.5), kind=kLoop, calls=%fused_computation | loop fusion | bytes 4194304 | tf_op jit(solution)/shard_map/slice | solution.py:315
  3.8 4.9 %collective-permute-start = (bf16[4096,128]{1,0:T(8,128)(2,1)}, bf16[4096,128]{1,0:T(8,128)(2,1)S(1)}, u32[]{:S(2)}, u32[]{:S(2)}) collective-permute-start(bf16[4096,128]{1,0:T(8,128)(2,1)} %get-tuple-element.3), channel_id=1, source_target_pairs={{0,4},{4,8},{8,12},{12,16},{16,20},{20,24},{24,28},{28,32},{32,36}... | collective-permute-start | bytes 3145736 | tf_op jit(solution)/shard_map/ppermute | solution.py:316
  8.7 1.9 %collective-permute-start.1 = (bf16[4096,128]{1,0:T(8,128)(2,1)}, bf16[4096,128]{1,0:T(8,128)(2,1)}, u32[]{:S(2)}, u32[]{:S(2)}) collective-permute-start(bf16[4096,128]{1,0:T(8,128)(2,1)} %get-tuple-element.2), channel_id=1, source_target_pairs={{4,0},{8,4},{12,8},{16,12},{20,16},{24,20},{28,24},{32,28},{36,32}... | collective-permute-start | bytes 3145736 | tf_op jit(solution)/shard_map/ppermute | solution.py:315
  10.7 0.0 copy-done.1
  10.7 0.0 copy-done.2
  10.7 0.0 copy-start
  10.7 3.4 %copy-done = bf16[1,16384,256]{2,1,0:T(8,128)(2,1)S(1)} copy-done((bf16[1,16384,256]{2,1,0:T(8,128)(2,1)S(1)}, bf16[1,16384,256]{2,1,0:T(8,128)(2,1)}, u32[]{:S(2)}) %copy-start) | copy-done | bytes 8388632
  14.1 6.3 %own_rows.1.before = f32[768,128]{1,0:T(8,128)S(1)} custom-call(s32[4]{0:T(128)S(1)} %bitcast.13, bf16[16384,256]{1,0:T(8,128)(2,1)S(1)} %bitcast.10, bf16[8192,128]{1,0:T(8,128)(2,1)S(1)} %bitcast.12), custom_call_target="tpu_custom_call" | custom-call | flops 2415919104 | bytes 10485760 | tf_op jit(solution)/shard_map/own_rows/pallas_call | solution.py:127
  20.4 0.3 collective-permute-done.from_prev
  20.8 4.4 %collective-permute-done.1.from_next = bf16[4096,128]{1,0:T(8,128)(2,1)} collective-permute-done((bf16[4096,128]{1,0:T(8,128)(2,1)}, bf16[4096,128]{1,0:T(8,128)(2,1)}, u32[]{:S(2)}, u32[]{:S(2)}) %collective-permute-start.1) | collective-permute-done | bytes 1048608 | tf_op jit(solution)/shard_map/ppermute | solution.py:315
  25.2 3.6 %edge_rows.1 = f32[768,128]{1,0:T(8,128)S(1)} custom-call(s32[4]{0:T(128)S(1)} %bitcast.14, bf16[16384,256]{1,0:T(8,128)(2,1)S(1)} %bitcast.11, bf16[4096,128]{1,0:T(8,128)(2,1)S(1)} %collective-permute-done.from_prev, bf16[4096,128]{1,0:T(8,128)(2,1)} %collective-permute-done.1.from_next, f32[768,128]{1,0:T(8,128)S(1)} %own_rows.1.before), custom_call_target="tpu_custom_call" | custom-call | flops 268435456 | bytes 6291456 | tf_op jit(solution)/shard_map/edge_rows/pallas_call | solution.py:154
  28.8 0.1 collective-permute-start.2
  28.9 1.4 %collective-permute-done.2 = f32[384,128]{1,0:T(8,128)S(1)} collective-permute-done((f32[384,128]{1,0:T(8,128)S(1)}, f32[384,128]{1,0:T(8,128)S(1)}, u32[]{:S(2)}, u32[]{:S(2)}) %collective-permute-start.2) | collective-permute-done | bytes 196640 | tf_op jit(solution)/shard_map/ppermute | solution.py:292
  30.4 15.6 %all_to_all.15 = f32[16,24,128]{2,1,0:T(8,128)S(1)} all-to-all(f32[16,24,128]{2,1,0:T(8,128)S(1)} %bitcast.17), channel_id=1, replica_groups=mesh['y'=4,'z'=8,'c'=2,'g'=4] {'y','g'}, dimensions={0} | all-to-all | bytes 393216 | tf_op jit(solution)/shard_map/all_to_all | solution.py:303
  46.0 15.1 %all_to_all.16 = f32[8,24,128]{2,1,0:T(8,128)S(1)} all-to-all(f32[8,24,128]{2,1,0:T(8,128)S(1)} %broadcast_in_dim.4), channel_id=1, replica_groups=mesh['y'=4,'z'=8,'c'=2,'g'=4] {'z'}, dimensions={0} | all-to-all | bytes 196608 | tf_op jit(solution)/shard_map/all_to_all | solution.py:288
  61.1 9.8 %all_to_all.17 = f32[16,24,128]{2,1,0:T(8,128)S(1)} all-to-all(f32[16,24,128]{2,1,0:T(8,128)S(1)} %broadcast_in_dim.5), channel_id=1, replica_groups=mesh['y'=4,'z'=8,'c'=2,'g'=4] {'y','g'}, dimensions={0} | all-to-all | bytes 393216 | tf_op jit(solution)/shard_map/all_to_all | solution.py:288
  70.9 0.0 copy-start.3
  70.9 4.2 %collective-permute-start.3 = (f32[384,128]{1,0:T(8,128)S(1)}, f32[384,128]{1,0:T(8,128)S(1)}, u32[]{:S(2)}, u32[]{:S(2)}) collective-permute-start(f32[384,128]{1,0:T(8,128)S(1)} %bitcast.15), channel_id=1, source_target_pairs={{0,4},{4,0},{1,5},{5,1},{2,6},{6,2},{3,7},{7,3},{8,12},{12,8},{9,1... | collective-permute-start | bytes 589832 | tf_op jit(solution)/shard_map/ppermute | solution.py:292
  75.2 1.1 %collective-permute-done.3.other = f32[384,128]{1,0:T(8,128)S(1)} collective-permute-done((f32[384,128]{1,0:T(8,128)S(1)}, f32[384,128]{1,0:T(8,128)S(1)}, u32[]{:S(2)}, u32[]{:S(2)}) %collective-permute-start.3) | collective-permute-done | bytes 196640 | tf_op jit(solution)/shard_map/ppermute | solution.py:292
  76.2 0.0 copy-start.4
  76.2 0.0 copy-done.3
  76.2 0.7 copy-done.4
  76.9 12.3 %factor_and_projection.1 = (f32[256,256]{1,0:T(8,128)}, f32[128,256]{1,0:T(8,128)}) custom-call(s32[1]{0:T(128)} %bitcast.core, f32[384,128]{1,0:T(8,128)} %bitcast.16, f32[384,128]{1,0:T(8,128)} %copy-done.4), custom_call_target="tpu_custom_call" | custom-call | tf_op jit(solution)/shard_map/factor_and_projection/pallas_call | solution.py:268
  (6 shorter events, 0.1 us)
Async XLA Ops:
  0.6 10.0 %copy-start.1 = (bf16[1,8192,128]{2,1,0:T(8,128)(2,1)S(1)}, bf16[1,8192,128]{2,1,0:T(8,128)(2,1)}, u32[]{:S(2)}) copy-start(bf16[1,8192,128]{2,1,0:T(8,128)(2,1)} %param.5) | copy-start | bytes 6291460
  0.6 10.0 %copy-start.2 = (s32[1,1,4]{2,1,0:T(1,128)S(1)}, s32[1,1,4]{2,1,0:T(1,128)}, u32[]{:S(2)}) copy-start(s32[1,1,4]{2,1,0:T(1,128)} %param.4) | copy-start | bytes 52
  3.8 17.0 %collective-permute-start = (bf16[4096,128]{1,0:T(8,128)(2,1)}, bf16[4096,128]{1,0:T(8,128)(2,1)S(1)}, u32[]{:S(2)}, u32[]{:S(2)}) collective-permute-start(bf16[4096,128]{1,0:T(8,128)(2,1)} %get-tuple-element.3), channel_id=1, source_target_pairs={{0,4},{4,8},{8,12},{12,16},{16,20},{20,24},{24,28},{28,32},{32,36}... | collective-permute-start | bytes 3145736 | tf_op jit(solution)/shard_map/ppermute | solution.py:316
  8.7 16.4 %collective-permute-start.1 = (bf16[4096,128]{1,0:T(8,128)(2,1)}, bf16[4096,128]{1,0:T(8,128)(2,1)}, u32[]{:S(2)}, u32[]{:S(2)}) collective-permute-start(bf16[4096,128]{1,0:T(8,128)(2,1)} %get-tuple-element.2), channel_id=1, source_target_pairs={{4,0},{8,4},{12,8},{16,12},{20,16},{24,20},{28,24},{32,28},{36,32}... | collective-permute-start | bytes 3145736 | tf_op jit(solution)/shard_map/ppermute | solution.py:315
  10.7 3.4 %copy-start = (bf16[1,16384,256]{2,1,0:T(8,128)(2,1)S(1)}, bf16[1,16384,256]{2,1,0:T(8,128)(2,1)}, u32[]{:S(2)}) copy-start(bf16[1,16384,256]{2,1,0:T(8,128)(2,1)} %param.3) | copy-start | bytes 25165828
  28.8 1.5 %collective-permute-start.2 = (f32[384,128]{1,0:T(8,128)S(1)}, f32[384,128]{1,0:T(8,128)S(1)}, u32[]{:S(2)}, u32[]{:S(2)}) collective-permute-start(f32[384,128]{1,0:T(8,128)S(1)} %constant_dynamic-slice_fusion), channel_id=1, source_target_pairs={{0,4},{4,0},{1,5},{5,1},{2,6},{6,2},{3,7},{7,3},{8,12},{12,8},{9,1... | collective-permute-start | bytes 589832 | tf_op jit(solution)/shard_map/ppermute | solution.py:292
  70.9 5.3 %copy-start.3 = (f32[16,24,128]{2,1,0:T(8,128)}, f32[16,24,128]{2,1,0:T(8,128)S(1)}, u32[]{:S(2)}) copy-start(f32[16,24,128]{2,1,0:T(8,128)S(1)} %all_to_all.17) | copy-start | bytes 589828
  70.9 5.3 %collective-permute-start.3 = (f32[384,128]{1,0:T(8,128)S(1)}, f32[384,128]{1,0:T(8,128)S(1)}, u32[]{:S(2)}, u32[]{:S(2)}) collective-permute-start(f32[384,128]{1,0:T(8,128)S(1)} %bitcast.15), channel_id=1, source_target_pairs={{0,4},{4,0},{1,5},{5,1},{2,6},{6,2},{3,7},{7,3},{8,12},{12,8},{9,1... | collective-permute-start | bytes 589832 | tf_op jit(solution)/shard_map/ppermute | solution.py:292
  76.2 0.7 copy-start.4

commit v2 on v1

v2 whole, which is shorter than its diff:
```python
import functools

import jax
import jax.numpy as jnp
from jax import lax
from jax.experimental import pallas as pl
from jax.experimental.pallas import tpu as pltpu
from jax.sharding import Mesh, PartitionSpec as P

BLOCK = 128
LANES = 128
MEMBERS = 256
MODES = 128
BLOCKS = 64
CHUNK = 16
CHUNK_ROWS = CHUNK * BLOCK
TILE = 8
STACK = 640
NEAR = 21
FAR = 11
NEAR_ROWS = NEAR * BLOCK
FAR_ROWS = FAR * BLOCK
PARCEL = 2 * FAR_ROWS
VMEM_BYTES = 51 * 1024 * 1024
EDGE_VMEM_BYTES = 45 * 1024 * 1024


def transposed_product(a, b):
    return lax.dot_general(a, b, (((0,), (0,)), ((), ())), preferred_element_type=jnp.float32)


def kept_blocks(values, first, start, stop):
    parts = []
    for index in range(values.shape[0] // BLOCK):
        part = values[index * BLOCK : (index + 1) * BLOCK, :]
        keep = (first + index >= start) & (first + index < stop)
        parts.append(jnp.where(keep, part, jnp.zeros_like(part)))
    return jnp.concatenate(parts, axis=0)


def block_rows(start, count):
    return pl.ds(pl.multiple_of(start * BLOCK, BLOCK), count * BLOCK)


def parcels_kernel(core, moves, panel, modes, to_inner, to_outer, sems):
    head, tail, prev, following = moves[0], moves[1], moves[2], moves[3]
    block_total = modes.shape[0] // BLOCK
    tail_start = head + block_total - prev - following
    second = core[0] != 0

    def far_copies(start, out, which):
        return [
            pltpu.make_async_copy(
                panel.at[block_rows(start, FAR), pl.ds(half * LANES, LANES)],
                out.at[pl.ds(half * FAR_ROWS, FAR_ROWS)],
                sems.at[which, half],
            )
            for half in range(2)
        ]

    def near_copies(start, out, which):
        return [
            pltpu.make_async_copy(
                modes.at[pl.ds(start * BLOCK, NEAR_ROWS)],
                out.at[pl.ds(0, NEAR_ROWS)],
                sems.at[which, 0],
            )
        ]

    choices = []
    for here, to_prev, to_next in (
        (second, to_inner, to_outer),
        (jnp.logical_not(second), to_outer, to_inner),
    ):
        choices += [
            (here & (head > 0), far_copies(0, to_prev, 0)),
            (here & (head == 0), near_copies(0, to_prev, 0)),
            (here & (tail > 0), far_copies(tail_start + NEAR, to_next, 1)),
            (here & (tail == 0), near_copies(block_total - NEAR, to_next, 1)),
        ]
    for chosen, copies in choices:

        @pl.when(chosen)
        def _():
            for copy in copies:
                copy.start()

    for chosen, copies in choices:

        @pl.when(chosen)
        def _():
            for copy in copies:
                copy.wait()


def own_rows_kernel(
    moves, panel, modes, out, panel_v, modes_v, gram, cross, panel_sem, modes_sem
):
    head, tail, prev, following = moves[0], moves[1], moves[2], moves[3]
    block_total = modes.shape[0] // BLOCK
    lead = block_total // 2
    own = block_total - prev - following
    valid = head + own + tail
    steps = jnp.maximum(lax.div(valid + (CHUNK - 1), CHUNK), 1)

    def panel_copy(i):
        rows = block_rows(i * CHUNK, CHUNK)
        return pltpu.make_async_copy(panel.at[rows], panel_v.at[rows], panel_sem.at[i])

    modes_copy = pltpu.make_async_copy(
        modes, modes_v.at[block_rows(lead + head - prev, block_total)], modes_sem
    )
    panel_copy(0).start()
    modes_copy.start()

    def launch(i, carry):
        panel_copy(i).start()
        return carry

    lax.fori_loop(1, steps, launch, 0)
    gram[...] = jnp.zeros_like(gram)
    cross[...] = jnp.zeros_like(cross)
    modes_copy.wait()

    def step(i, carry):
        panel_copy(i).wait()
        block = i * CHUNK
        values = panel_v[block_rows(block, CHUNK), :]
        beside = modes_v[block_rows(block + lead, CHUNK), :]
        gram[...] += transposed_product(values, kept_blocks(values, block, 0, valid))
        cross[...] += transposed_product(kept_blocks(beside, block, head, head + own), values)
        return carry

    lax.fori_loop(0, steps, step, 0)
    out[:LANES, :] = gram[:LANES, :LANES]
    out[LANES : 2 * LANES, :] = gram[:LANES, LANES:]
    out[2 * LANES : 3 * LANES, :] = gram[LANES:, LANES:]
    for i in range(2):
        out[(3 + i) * LANES : (4 + i) * LANES, :] = cross[:, i * LANES : (i + 1) * LANES]


class Edge:
    def __init__(self, from_prev, moves, block_total):
        head, tail, prev, following = moves[0], moves[1], moves[2], moves[3]
        own = block_total - prev - following
        far_start = jnp.minimum(block_total - following, block_total - FAR)
        self.near = jnp.where(from_prev, head, tail)
        self.near_source = jnp.where(from_prev, jnp.maximum(head - NEAR, 0), head + own)
        self.near_offset = jnp.where(from_prev, jnp.minimum(head, NEAR), NEAR)
        self.near_first = jnp.where(from_prev, NEAR - head, 0)
        self.near_stop = jnp.where(from_prev, NEAR, tail)
        self.far = jnp.where(from_prev, prev, following) - NEAR
        self.far_source = jnp.where(from_prev, NEAR, far_start)

    def copies(self, panel, modes, near_v, far_v, sems):
        near = pltpu.make_async_copy(
            panel.at[block_rows(self.near_source, NEAR)],
            near_v.at[pl.ds(NEAR_ROWS, NEAR_ROWS)],
            sems.at[0],
        )
        far = pltpu.make_async_copy(
            modes.at[block_rows(self.far_source, FAR)], far_v, sems.at[1]
        )
        return [(self.near > 0, near), (self.far > 0, far)]

    def multiply(self, near_v, far_v, parcel, out):
        def add(index, values):
            out[index * LANES : (index + 1) * LANES, :] += values

        @pl.when(self.near > 0)
        def _():
            mode_values = kept_blocks(parcel[:NEAR_ROWS, :], 0, self.near_first, self.near_stop)
            panel_values = near_v[block_rows(self.near_offset, NEAR), :]
            product = transposed_product(mode_values, panel_values)
            for i in range(2):
                add(3 + i, product[:, i * LANES : (i + 1) * LANES])

        @pl.when(self.far > 0)
        def _():
            mode_values = kept_blocks(far_v[...], 0, 0, self.far)
            for i in range(2):
                values = parcel[i * FAR_ROWS : (i + 1) * FAR_ROWS, :]
                add(3 + i, transposed_product(mode_values, values))


def inner_edge_kernel(
    core, moves, panel, modes, parcel, before, out, outer_near, outer_far, near_v, far_v, sems
):
    block_total = modes.shape[0] // BLOCK
    inner = Edge(core[0] != 0, moves, block_total)
    outer = Edge(core[0] == 0, moves, block_total)
    inner_copies = inner.copies(panel, modes, near_v, far_v, sems.at[0])
    outer_copies = outer.copies(panel, modes, outer_near, outer_far, sems.at[1])
    for needed, copy in inner_copies + outer_copies:
        pl.when(needed)(copy.start)
    filler = jnp.zeros((NEAR_ROWS, MEMBERS), near_v.dtype)
    near_v[:NEAR_ROWS, :] = filler
    outer_near[:NEAR_ROWS, :] = filler
    out[...] = before[...]
    for needed, copy in inner_copies:
        pl.when(needed)(copy.wait)
    inner.multiply(near_v, far_v, parcel, out)
    for needed, copy in outer_copies:
        pl.when(needed)(copy.wait)


def outer_edge_kernel(core, moves, outer_near, outer_far, parcel, before, out):
    outer = Edge(core[0] == 0, moves, BLOCKS)
    out[...] = before[...]
    outer.multiply(outer_near, outer_far, parcel, out)


SMEM = pl.BlockSpec(memory_space=pltpu.SMEM)
VMEM = pl.BlockSpec(memory_space=pltpu.VMEM)
HBM = pl.BlockSpec(memory_space=pltpu.HBM)


def parcels(core, moves, panel, modes):
    parcel = jax.ShapeDtypeStruct((PARCEL, LANES), modes.dtype)
    return pl.pallas_call(
        parcels_kernel,
        out_shape=(parcel, parcel),
        in_specs=[SMEM, SMEM, HBM, HBM],
        out_specs=(VMEM, VMEM),
        scratch_shapes=[pltpu.SemaphoreType.DMA((2, 2))],
        compiler_params=pltpu.CompilerParams(vmem_limit_bytes=VMEM_BYTES),
        cost_estimate=pl.CostEstimate(flops=0, bytes_accessed=3 * 1024 * 1024, transcendentals=0),
        name="parcels",
    )(core, moves, panel, modes)


def own_rows(moves, panel, modes):
    slots = panel.shape[0] // BLOCK
    return pl.pallas_call(
        own_rows_kernel,
        out_shape=jax.ShapeDtypeStruct((STACK, LANES), jnp.float32),
        in_specs=[SMEM, HBM, HBM],
        out_specs=VMEM,
        scratch_shapes=[
            pltpu.VMEM(panel.shape, panel.dtype),
            pltpu.VMEM((panel.shape[0] + modes.shape[0] // 2, MODES), modes.dtype),
            pltpu.VMEM((MEMBERS, MEMBERS), jnp.float32),
            pltpu.VMEM((MODES, MEMBERS), jnp.float32),
            pltpu.SemaphoreType.DMA((slots // CHUNK,)),
            pltpu.SemaphoreType.DMA,
        ],
        compiler_params=pltpu.CompilerParams(vmem_limit_bytes=VMEM_BYTES),
        cost_estimate=pl.CostEstimate(
            flops=2 * 12288 * 384 * 256, bytes_accessed=10 * 1024 * 1024, transcendentals=0
        ),
        name="own_rows",
    )(moves, panel, modes)


def inner_edge(core, moves, panel, modes, parcel, before):
    near = (2 * NEAR_ROWS, MEMBERS)
    far = (FAR_ROWS, MODES)
    return pl.pallas_call(
        inner_edge_kernel,
        out_shape=(
            jax.ShapeDtypeStruct((STACK, LANES), jnp.float32),
            jax.ShapeDtypeStruct(near, panel.dtype),
            jax.ShapeDtypeStruct(far, modes.dtype),
        ),
        in_specs=[SMEM, SMEM, HBM, HBM, VMEM, VMEM],
        out_specs=(VMEM, VMEM, VMEM),
        scratch_shapes=[
            pltpu.VMEM(near, panel.dtype),
            pltpu.VMEM(far, modes.dtype),
            pltpu.SemaphoreType.DMA((2, 2)),
        ],
        compiler_params=pltpu.CompilerParams(vmem_limit_bytes=EDGE_VMEM_BYTES),
        cost_estimate=pl.CostEstimate(
            flops=2 * 2048 * 128 * 256, bytes_accessed=4 * 1024 * 1024, transcendentals=0
        ),
        name="inner_edge",
    )(core, moves, panel, modes, parcel, before)


def outer_edge(core, moves, near, far, parcel, before):
    return pl.pallas_call(
        outer_edge_kernel,
        out_shape=jax.ShapeDtypeStruct((STACK, LANES), jnp.float32),
        in_specs=[SMEM, SMEM, VMEM, VMEM, VMEM, VMEM],
        out_specs=VMEM,
        compiler_params=pltpu.CompilerParams(vmem_limit_bytes=EDGE_VMEM_BYTES),
        cost_estimate=pl.CostEstimate(
            flops=2 * 2048 * 128 * 256, bytes_accessed=2 * 1024 * 1024, transcendentals=0
        ),
        name="outer_edge",
    )(core, moves, near, far, parcel, before)


def projected(product, inverse_t):
    high = product.astype(jnp.bfloat16)
    rest = product - high.astype(jnp.float32)
    middle = rest.astype(jnp.bfloat16)
    low = (rest - middle.astype(jnp.float32)).astype(jnp.bfloat16)

    def part(values):
        return lax.dot_general(
            values, inverse_t, (((1,), (1,)), ((), ())), preferred_element_type=jnp.float32
        )

    return part(low) + part(middle) + part(high)


def factor_kernel(stack, factor, projection, work, packed, cross):
    squares = [stack[i * LANES : (i + 1) * LANES, :] for i in range(STACK // LANES)]
    work[:LANES, :LANES] = squares[0]
    work[:LANES, LANES:] = squares[1]
    work[LANES:, :LANES] = squares[1].T
    work[LANES:, LANES:] = squares[2]
    cross[:, :LANES] = squares[3]
    cross[:, LANES:] = squares[4]

    size = MEMBERS
    lanes = lax.broadcasted_iota(jnp.int32, (TILE, LANES), 1)
    subs = lax.broadcasted_iota(jnp.int32, (TILE, LANES), 0)
    groups = size // TILE
    halves = size // LANES

    def row_of(values, r):
        return jnp.broadcast_to(values[r : r + 1, :], (TILE, LANES))

    def column_of(values, c):
        return jnp.broadcast_to(values[:, c : c + 1], (TILE, LANES))

    def loaded(i):
        return [work[i * TILE : (i + 1) * TILE, h * LANES : (h + 1) * LANES] for h in range(halves)]

    def reduced(old, before):
        half, start, solved_rows = before
        fresh = list(old)
        inside = (lanes >= start) & (lanes < start + TILE)
        fresh[half] = jnp.where(inside, 0.0, old[half])
        for q in range(TILE):
            coefficient = column_of(old[half], start + q)
            for h in range(halves):
                fresh[h] = fresh[h] - coefficient * solved_rows[q][h]
        return fresh

    def bf16_parts(values, order):
        parts = []
        for _ in range(3):
            part = values.astype(jnp.bfloat16).astype(jnp.float32)
            parts.append(part)
            values = values - part
        return jnp.concatenate([parts[k] for k in order], axis=0).astype(jnp.bfloat16)

    before = None
    for group in range(groups):
        half, start = divmod(group * TILE, LANES)
        panel = loaded(group)
        if before is not None:
            panel = reduced(panel, before)
        raw = list(panel)
        columns = [column_of(panel[half], start + r) for r in range(TILE)]
        below = list(range(group + 1, groups)) if before is not None else []
        for r in range(TILE):
            column = columns[r]
            at_row = subs == r
            at_lane = lanes == start + r
            recip = 1.0 / row_of(column, r)
            scale = lax.rsqrt(row_of(column, r))
            factor_of = jnp.where(at_row, -1.0, column)
            for s in range(r + 1, TILE):
                kept = jnp.where(at_row, 0.0, columns[s])
                columns[s] = kept - (factor_of * row_of(columns[s], r)) * recip
            index = group * TILE + r
            for h in range(halves):
                row = row_of(panel[h], r)
                kept = jnp.where(at_row, 0.0, panel[h])
                if h == half:
                    row = jnp.where(at_lane, 1.0, row)
                    kept = jnp.where(at_lane, 0.0, kept)
                packed[index : index + 1, h * LANES : (h + 1) * LANES] = (row * scale)[0:1]
                panel[h] = kept - (factor_of * row) * recip
            for i in below[r::TILE]:
                fresh = loaded(i)
                inside = (lanes >= before[1]) & (lanes < before[1] + TILE)
                fresh[before[0]] = jnp.where(inside, 0.0, fresh[before[0]])
                for h in range(halves):
                    part = update[i * TILE - first : (i + 1) * TILE - first, h * LANES : (h + 1) * LANES]
                    work[i * TILE : (i + 1) * TILE, h * LANES : (h + 1) * LANES] = fresh[h] - part
        before = (half, start, [[row_of(panel[h], q) for h in range(halves)] for q in range(TILE)])
        first = half * LANES
        left = bf16_parts(jnp.concatenate(raw[half:], axis=1), (0, 0, 0, 1, 1, 2))
        right = bf16_parts(jnp.concatenate(panel, axis=1), (0, 1, 2, 0, 1, 0))
        update = transposed_product(left, right)

    row = lax.broadcasted_iota(jnp.int32, (size, size), 0)
    column = lax.broadcasted_iota(jnp.int32, (size, size), 1)
    result = packed[...]
    factor[...] = jnp.where(
        column > row, result, jnp.where(column == row, 1.0 / result, jnp.zeros_like(result))
    )
    inverse_t = jnp.where(column <= row, result, jnp.zeros_like(result)).astype(jnp.bfloat16)
    projection[...] = projected(cross[...], inverse_t)


def factor_and_projection(stack):
    return pl.pallas_call(
        factor_kernel,
        out_shape=(
            jax.ShapeDtypeStruct((MEMBERS, MEMBERS), jnp.float32),
            jax.ShapeDtypeStruct((MODES, MEMBERS), jnp.float32),
        ),
        in_specs=[VMEM],
        out_specs=(VMEM, VMEM),
        scratch_shapes=[
            pltpu.VMEM((MEMBERS, MEMBERS), jnp.float32),
            pltpu.VMEM((MEMBERS, MEMBERS), jnp.float32),
            pltpu.VMEM((MODES, MEMBERS), jnp.float32),
        ],
        name="factor_and_projection",
    )(stack)


def to_all(values, axes):
    count = lax.axis_size(axes)
    copies = jnp.broadcast_to(values[None], (count,) + values.shape)
    return lax.all_to_all(copies, axes, 0, 0)


def summed(stack):
    axes = ("y", "g")
    count = lax.axis_size(axes)
    pieces = stack.reshape(count, stack.shape[0] // count, LANES)
    piece = lax.all_to_all(pieces, axes, 0, 0).sum(0)
    piece = piece + lax.ppermute(piece, "c", [(0, 1), (1, 0)])
    piece = to_all(piece, "z").sum(0)
    return to_all(piece, axes).reshape(stack.shape)


def body(sensitivity, block_moves, shape_modes):
    panel = sensitivity[0]
    modes = shape_modes[0]
    moves = block_moves[0, 0]
    core = lax.axis_index("c").astype(jnp.int32).reshape(1)
    chain = ("y", "z", "c")
    count = lax.axis_size(chain)
    to_inner, to_outer = parcels(core, moves, panel, modes)
    pairs = range(1, count - 1, 2)
    outer = lax.ppermute(
        to_outer, chain, [(i, i + 1) for i in pairs] + [(i + 1, i) for i in pairs]
    )
    inner = lax.ppermute(to_inner, chain, [(i, i ^ 1) for i in range(count)])
    stack = own_rows(moves, panel, modes)
    stack, near, far = inner_edge(core, moves, panel, modes, inner, stack)
    stack = outer_edge(core, moves, near, far, outer, stack)
    return factor_and_projection(summed(stack))


def solution(mesh):
    split = Mesh(mesh.devices.reshape(4, 8, 2, 4), ("y", "z", "c", "g"))
    spec = P("g", ("y", "z", "c"), None)
    return jax.shard_map(
        body, mesh=split, in_specs=(spec, spec, spec), out_specs=(P(), P()), check_vma=False
    )
```

time: 89.4 us -> 74.4 us (0.83)
  local copies, waits for them, and re-layouts: 7.26 us -> 0.69 us
  Pallas kernels: 22.3 us -> 18.2 us
  blocking collectives: 40.5 us -> 38 us
  waiting for transfers between devices: 7.24 us -> 5.09 us
    pallas_call x1, Pallas kernels: 12.3 us -> 8.84 us  [factor_and_projection(): pl.pallas_call(factor_kernel, out_shape=(jax.ShapeDtypeStruct((MEMBERS, M...]
    unnamed x10 -> x4, local copies, waits for them, and re-layouts: 4.06 us -> 0.65 us
    slice x1 -> x0, local copies, waits for them, and re-layouts: 3.15 us -> none  [body(): modes[:edge]]
    all_to_all x1, blocking collectives: 15.6 us -> 13 us  [summed(): piece = lax.all_to_all(pieces, axes, 0, 0).sum(0)]
    ppermute x4 -> x3, waiting for transfers between devices: 7.24 us -> 5.09 us  [the longest x1 4.25 us: body(): lax.ppermute(to_outer, chain, [(i, i + 1) for i in pairs] + [(i + 1, i) f...]
    pallas_call x1, Pallas kernels: 6.34 us -> 4.32 us  [own_rows(): pl.pallas_call(own_rows_kernel, out_shape=jax.ShapeDtypeStruct((STACK, LA...]
    pallas_call x1 -> x3, Pallas kernels: 3.59 us -> 5.02 us  [the longest x1 2.08 us: inner_edge(): pl.pallas_call(inner_edge_kernel, out_shape=(jax.ShapeDtypeStruct((STACK,...]
    ppermute x4 -> x3, starting transfers between devices: 11.2 us -> 10.7 us  [the longest x1 5.45 us: summed(): piece = piece + lax.ppermute(piece, 'c', [(0, 1), (1, 0)])]
  transfers between devices with their start and end apart: 4 -> 3, of which waited for: 4 -> 2; matrix products, arithmetic and copies ran while one was open for 0% -> 0% of each run, Pallas kernels for 7% -> 9%
where the time goes in v2:
time: 74.4 us; the launch traced here: 73.4 us
  blocking collectives  38 us (51%)
  Pallas kernels  18.2 us (24%)
  starting transfers between devices  10.7 us (14%)
  waiting for transfers between devices  5.09 us (7%)
    all_to_all x2, blocking collectives, to_all(): return lax.all_to_all(copies, axes, 0, 0)  24.9 us
    all_to_all x1, blocking collectives, summed(): piece = lax.all_to_all(pieces, axes, 0, 0).sum(0)  13 us
    pallas_call x1, Pallas kernels, factor_and_projection(): pl.pallas_call(factor_kernel, out_shape=(jax.ShapeDtypeStruct((MEMBERS, M...  8.84 us
    ppermute x1, starting transfers between devices, summed(): piece = piece + lax.ppermute(piece, 'c', [(0, 1), (1, 0)])  5.45 us
    pallas_call x1, Pallas kernels, own_rows(): pl.pallas_call(own_rows_kernel, out_shape=jax.ShapeDtypeStruct((STACK, LA...  4.32 us
    ppermute x1, waiting for transfers between devices, body(): lax.ppermute(to_outer, chain, [(i, i + 1) for i in pairs] + [(i + 1, i) f...  4.25 us
    ppermute x1, starting transfers between devices, body(): inner = lax.ppermute(to_inner, chain, [(i, i ^ 1) for i in range(count)])  3.33 us
    pallas_call x1, Pallas kernels, inner_edge(): pl.pallas_call(inner_edge_kernel, out_shape=(jax.ShapeDtypeStruct((STACK,...  2.08 us
  transfers between devices with their start and end apart: 3, of which 2 were waited for; matrix products, arithmetic and copies ran while one was open for 0% of the time, Pallas kernels for 9%

profile of v2, /device:TPU:1, one launch (start us, length us, event | category | flops | bytes accessed | tf_op | source)
XLA Modules:
  0.0 73.4 jit_solution(14642337534507965992)
XLA Ops:
  0.6 0.0 copy-start.1
  0.6 0.6 copy-done.1
  1.3 0.0 copy-start
  1.3 2.0 %parcels.1 = (bf16[2816,128]{1,0:T(8,128)(2,1)S(1)}, bf16[2816,128]{1,0:T(8,128)(2,1)S(1)}) custom-call(s32[1]{0:T(128)} %bitcast.core, s32[4]{0:T(128)S(1)} %bitcast.10, bf16[16384,256]{1,0:T(8,128)(2,1)} %bitcast.14, bf16[8192,128]{1,0:T(8,128)(2,1)} %bitcast.6), custom_call_target="tpu_custom_call" | custom-call | bytes 3145728 | tf_op jit(solution)/shard_map/parcels/pallas_call | solution.py:220
  3.3 3.3 %collective-permute-start = (bf16[2816,128]{1,0:T(8,128)(2,1)S(1)}, bf16[2816,128]{1,0:T(8,128)(2,1)S(1)}, u32[]{:S(2)}, u32[]{:S(2)}) collective-permute-start(bf16[2816,128]{1,0:T(8,128)(2,1)S(1)} %get-tuple-element.7), channel_id=1, source_target_pairs={{0,4},{4,0},{8,12},{12,8},{16,20},{20,16},{24,28},{28,24},{32,36},... | collective-permute-start | bytes 2162696 | tf_op jit(solution)/shard_map/ppermute | solution.py:448
  6.6 1.9 %collective-permute-start.1 = (bf16[2816,128]{1,0:T(8,128)(2,1)S(1)}, bf16[2816,128]{1,0:T(8,128)(2,1)S(1)}, u32[]{:S(2)}, u32[]{:S(2)}) collective-permute-start(bf16[2816,128]{1,0:T(8,128)(2,1)S(1)} %get-tuple-element.10), channel_id=1, source_target_pairs={{4,8},{12,16},{20,24},{28,32},{36,40},{44,48},{52,56},{60,64},{68,... | collective-permute-start | bytes 2162696 | tf_op jit(solution)/shard_map/ppermute | solution.py:445
  8.5 0.0 copy-done
  8.5 4.3 %own_rows.1.before = f32[640,128]{1,0:T(8,128)S(1)} custom-call(s32[4]{0:T(128)S(1)} %bitcast.11, bf16[16384,256]{1,0:T(8,128)(2,1)} %bitcast.15, bf16[8192,128]{1,0:T(8,128)(2,1)S(1)} %bitcast.7), custom_call_target="tpu_custom_call" | custom-call | flops 2415919104 | bytes 10485760 | tf_op jit(solution)/shard_map/own_rows/pallas_call | solution.py:234
  12.8 0.0 collective-permute-done.parcel
  12.9 2.1 %inner_edge.1 = (f32[640,128]{1,0:T(8,128)S(1)}, bf16[5376,256]{1,0:T(8,128)(2,1)S(1)}, bf16[1408,128]{1,0:T(8,128)(2,1)S(1)}) custom-call(s32[1]{0:T(128)} %bitcast.core, s32[4]{0:T(128)S(1)} %bitcast.12, bf16[16384,256]{1,0:T(8,128)(2,1)} %bitcast.16, bf16[8192,128]{1,0:T(8,128)(2,1)S(1)} %bitcast.8, bf16[2816,128]{1,0:T(8,128)(2,1)S(1)} %collective-permute-done.parcel, ...), custom_call_target="tpu_custom_call" | custom-call | flops 134217728 | bytes 4194304 | tf_op jit(solution)/shard_map/inner_edge/pallas_call | solution.py:258
  14.9 4.2 %collective-permute-done.1.parcel = bf16[2816,128]{1,0:T(8,128)(2,1)S(1)} collective-permute-done((bf16[2816,128]{1,0:T(8,128)(2,1)S(1)}, bf16[2816,128]{1,0:T(8,128)(2,1)S(1)}, u32[]{:S(2)}, u32[]{:S(2)}) %collective-permute-start.1) | collective-permute-done | bytes 720928 | tf_op jit(solution)/shard_map/ppermute | solution.py:445
  19.2 1.0 %outer_edge.1 = f32[640,128]{1,0:T(8,128)S(1)} custom-call(s32[1]{0:T(128)} %bitcast.core, s32[4]{0:T(128)S(1)} %bitcast.13, bf16[5376,256]{1,0:T(8,128)(2,1)S(1)} %get-tuple-element.8.outer_near, bf16[1408,128]{1,0:T(8,128)(2,1)S(1)} %get-tuple-element.9.outer_far, bf16[2816,128]{1,0:T(8,128)(2,1)S(1)} %collective-permute-done.1.parcel, ...), custom_call_target="tpu_custom_call" | custom-call | flops 134217728 | bytes 2097152 | tf_op jit(solution)/shard_map/outer_edge/pallas_call | solution.py:281
  20.2 13.0 %all_to_all.15 = f32[16,40,128]{2,1,0:T(8,128)S(1)} all-to-all(f32[16,40,128]{2,1,0:T(8,128)S(1)} %bitcast.9), channel_id=1, replica_groups=mesh['y'=4,'z'=8,'c'=2,'g'=4] {'y','g'}, dimensions={0} | all-to-all | bytes 655360 | tf_op jit(solution)/shard_map/all_to_all | solution.py:430
  33.2 5.5 %collective-permute-start.2 = (f32[40,128]{1,0:T(8,128)S(1)}, f32[40,128]{1,0:T(8,128)S(1)}, u32[]{:S(2)}, u32[]{:S(2)}) collective-permute-start(f32[40,128]{1,0:T(8,128)S(1)} %reduce_sum.18), channel_id=1, source_target_pairs={{0,4},{4,0},{1,5},{5,1},{2,6},{6,2},{3,7},{7,3},{8,12},{12,8},{9,1... | collective-permute-start | bytes 61448 | tf_op jit(solution)/shard_map/ppermute | solution.py:431
  38.7 0.8 %collective-permute-done.2 = f32[40,128]{1,0:T(8,128)S(1)} collective-permute-done((f32[40,128]{1,0:T(8,128)S(1)}, f32[40,128]{1,0:T(8,128)S(1)}, u32[]{:S(2)}, u32[]{:S(2)}) %collective-permute-start.2) | collective-permute-done | bytes 20512 | tf_op jit(solution)/shard_map/ppermute | solution.py:431
  39.5 13.7 %all_to_all.16 = f32[8,40,128]{2,1,0:T(8,128)S(1)} all-to-all(f32[8,40,128]{2,1,0:T(8,128)S(1)} %broadcast_in_dim.4), channel_id=1, replica_groups=mesh['y'=4,'z'=8,'c'=2,'g'=4] {'z'}, dimensions={0} | all-to-all | bytes 327680 | tf_op jit(solution)/shard_map/all_to_all | solution.py:423
  53.3 11.2 %all_to_all.17 = f32[16,40,128]{2,1,0:T(8,128)} all-to-all(f32[16,40,128]{2,1,0:T(8,128)S(1)} %broadcast_in_dim.5), channel_id=1, replica_groups=mesh['y'=4,'z'=8,'c'=2,'g'=4] {'y','g'}, dimensions={0} | all-to-all | bytes 655360 | tf_op jit(solution)/shard_map/all_to_all | solution.py:423
  64.5 8.8 %factor_and_projection.1 = (f32[256,256]{1,0:T(8,128)}, f32[128,256]{1,0:T(8,128)}) custom-call(f32[640,128]{1,0:T(8,128)} %bitcast.17), custom_call_target="tpu_custom_call" | custom-call | tf_op jit(solution)/shard_map/factor_and_projection/pallas_call | solution.py:403
  (5 shorter events, 0.1 us)
Async XLA Ops:
  0.6 0.7 copy-start.1
  1.3 7.2 %copy-start = (bf16[1,8192,128]{2,1,0:T(8,128)(2,1)S(1)}, bf16[1,8192,128]{2,1,0:T(8,128)(2,1)}, u32[]{:S(2)}) copy-start(bf16[1,8192,128]{2,1,0:T(8,128)(2,1)} %param.5) | copy-start | bytes 6291460
  3.3 9.6 %collective-permute-start = (bf16[2816,128]{1,0:T(8,128)(2,1)S(1)}, bf16[2816,128]{1,0:T(8,128)(2,1)S(1)}, u32[]{:S(2)}, u32[]{:S(2)}) collective-permute-start(bf16[2816,128]{1,0:T(8,128)(2,1)S(1)} %get-tuple-element.7), channel_id=1, source_target_pairs={{0,4},{4,0},{8,12},{12,8},{16,20},{20,16},{24,28},{28,24},{32,36},... | collective-permute-start | bytes 2162696 | tf_op jit(solution)/shard_map/ppermute | solution.py:448
  6.6 12.6 %collective-permute-start.1 = (bf16[2816,128]{1,0:T(8,128)(2,1)S(1)}, bf16[2816,128]{1,0:T(8,128)(2,1)S(1)}, u32[]{:S(2)}, u32[]{:S(2)}) collective-permute-start(bf16[2816,128]{1,0:T(8,128)(2,1)S(1)} %get-tuple-element.10), channel_id=1, source_target_pairs={{4,8},{12,16},{20,24},{28,32},{36,40},{44,48},{52,56},{60,64},{68,... | collective-permute-start | bytes 2162696 | tf_op jit(solution)/shard_map/ppermute | solution.py:445
  33.2 6.3 %collective-permute-start.2 = (f32[40,128]{1,0:T(8,128)S(1)}, f32[40,128]{1,0:T(8,128)S(1)}, u32[]{:S(2)}, u32[]{:S(2)}) collective-permute-start(f32[40,128]{1,0:T(8,128)S(1)} %reduce_sum.18), channel_id=1, source_target_pairs={{0,4},{4,0},{1,5},{5,1},{2,6},{6,2},{3,7},{7,3},{8,12},{12,8},{9,1... | collective-permute-start | bytes 61448 | tf_op jit(solution)/shard_map/ppermute | solution.py:431

commit v3 on v2

--- a/solution.py
+++ b/solution.py
@@ -14,7 +14,8 @@
 BLOCKS = 64
 CHUNK = 16
 CHUNK_ROWS = CHUNK * BLOCK
-TILE = 8
+SUBLANES = 8
+TILE = 16
 STACK = 640
 NEAR = 21
 FAR = 11
@@ -315,30 +316,24 @@
     cross[:, LANES:] = squares[4]
 
     size = MEMBERS
-    lanes = lax.broadcasted_iota(jnp.int32, (TILE, LANES), 1)
-    subs = lax.broadcasted_iota(jnp.int32, (TILE, LANES), 0)
+    lanes = lax.broadcasted_iota(jnp.int32, (SUBLANES, LANES), 1)
+    subs = lax.broadcasted_iota(jnp.int32, (SUBLANES, LANES), 0)
     groups = size // TILE
-    halves = size // LANES
-
-    def row_of(values, r):
-        return jnp.broadcast_to(values[r : r + 1, :], (TILE, LANES))
-
-    def column_of(values, c):
-        return jnp.broadcast_to(values[:, c : c + 1], (TILE, LANES))
+    halves = range(size // LANES)
+    tiles = range(TILE // SUBLANES)
+
+    def row_of(part, r):
+        return jnp.broadcast_to(part[r : r + 1, :], (SUBLANES, LANES))
+
+    def column_of(part, c):
+        return jnp.broadcast_to(part[:, c : c + 1], (SUBLANES, LANES))
+
+    def place_of(i, tile, half):
+        start = i * TILE + tile * SUBLANES
+        return slice(start, start + SUBLANES), slice(half * LANES, (half + 1) * LANES)
 
     def loaded(i):
-        return [work[i * TILE : (i + 1) * TILE, h * LANES : (h + 1) * LANES] for h in range(halves)]
-
-    def reduced(old, before):
-        half, start, solved_rows = before
-        fresh = list(old)
-        inside = (lanes >= start) & (lanes < start + TILE)
-        fresh[half] = jnp.where(inside, 0.0, old[half])
-        for q in range(TILE):
-            coefficient = column_of(old[half], start + q)
-            for h in range(halves):
-                fresh[h] = fresh[h] - coefficient * solved_rows[q][h]
-        return fresh
+        return [[work[place_of(i, t, h)] for h in halves] for t in tiles]
 
     def bf16_parts(values, order):
         parts = []
@@ -348,46 +343,114 @@
             values = values - part
         return jnp.concatenate([parts[k] for k in order], axis=0).astype(jnp.bfloat16)
 
-    before = None
+    def whole(panel, first):
+        return jnp.concatenate(
+            [jnp.concatenate(panel[t][first:], axis=1) for t in tiles], axis=0
+        )
+
+    def cleared(part, start, count):
+        return jnp.where((lanes >= start) & (lanes < start + count), 0.0, part)
+
+    def total_of(terms):
+        while len(terms) > 1:
+            paired = [terms[k] + terms[k + 1] for k in range(0, len(terms) - 1, 2)]
+            terms = paired + terms[len(terms) // 2 * 2 :]
+        return terms[0]
+
+    panel = loaded(0)
+    update = None
     for group in range(groups):
         half, start = divmod(group * TILE, LANES)
-        panel = loaded(group)
-        if before is not None:
-            panel = reduced(panel, before)
-        raw = list(panel)
-        columns = [column_of(panel[half], start + r) for r in range(TILE)]
-        below = list(range(group + 1, groups)) if before is not None else []
-        for r in range(TILE):
-            column = columns[r]
-            at_row = subs == r
-            at_lane = lanes == start + r
-            recip = 1.0 / row_of(column, r)
-            scale = lax.rsqrt(row_of(column, r))
-            factor_of = jnp.where(at_row, -1.0, column)
-            for s in range(r + 1, TILE):
-                kept = jnp.where(at_row, 0.0, columns[s])
-                columns[s] = kept - (factor_of * row_of(columns[s], r)) * recip
-            index = group * TILE + r
-            for h in range(halves):
-                row = row_of(panel[h], r)
-                kept = jnp.where(at_row, 0.0, panel[h])
-                if h == half:
-                    row = jnp.where(at_lane, 1.0, row)
-                    kept = jnp.where(at_lane, 0.0, kept)
-                packed[index : index + 1, h * LANES : (h + 1) * LANES] = (row * scale)[0:1]
-                panel[h] = kept - (factor_of * row) * recip
-            for i in below[r::TILE]:
-                fresh = loaded(i)
-                inside = (lanes >= before[1]) & (lanes < before[1] + TILE)
-                fresh[before[0]] = jnp.where(inside, 0.0, fresh[before[0]])
-                for h in range(halves):
-                    part = update[i * TILE - first : (i + 1) * TILE - first, h * LANES : (h + 1) * LANES]
-                    work[i * TILE : (i + 1) * TILE, h * LANES : (h + 1) * LANES] = fresh[h] - part
-        before = (half, start, [[row_of(panel[h], q) for h in range(halves)] for q in range(TILE)])
-        first = half * LANES
-        left = bf16_parts(jnp.concatenate(raw[half:], axis=1), (0, 0, 0, 1, 1, 2))
-        right = bf16_parts(jnp.concatenate(panel, axis=1), (0, 1, 2, 0, 1, 0))
-        update = transposed_product(left, right)
+        below = list(range(group + 1, groups))
+        columns = [
+            [[column_of(panel[t][half], start + r) for t in tiles] for r in range(SUBLANES)],
+            [[column_of(panel[1][half], start + SUBLANES + r)] for r in range(SUBLANES)],
+        ]
+
+        def lowered(i):
+            old = loaded(i)
+            if update is None:
+                return old
+            values, first, last_half, last_start = update
+            for t in tiles:
+                for h in halves:
+                    rows, cols = place_of(i, t, h)
+                    if h == last_half:
+                        old[t][h] = cleared(old[t][h], last_start, TILE)
+                    old[t][h] = old[t][h] - values[rows.start - first : rows.stop - first, cols]
+            return old
+
+        following = lowered(below[0]) if below else None
+        left = []
+        right = []
+        for tile in tiles:
+            origin = start + tile * SUBLANES
+            if below:
+                entries = [
+                    [column_of(following[t][half], origin + q) for t in tiles]
+                    for q in range(SUBLANES)
+                ]
+            left.append(list(panel[tile]))
+            taken = []
+            for r in range(SUBLANES):
+                column = columns[tile][r]
+                at_row = subs == r
+                at_lane = lanes == origin + r
+                pivot = row_of(column[0], r)
+                recip = 1.0 / pivot
+                scale = lax.rsqrt(pivot)
+                factor_of = [jnp.where(at_row, -1.0, column[0])] + column[1:]
+                taken.append((column[-1], recip))
+
+                def eliminated(parts, row):
+                    kept = [jnp.where(at_row, 0.0, parts[0])] + parts[1:]
+                    return [k - (f * row) * recip for k, f in zip(kept, factor_of)]
+
+                for s in range(r + 1, SUBLANES):
+                    columns[tile][s] = eliminated(columns[tile][s], row_of(columns[tile][s][0], r))
+                index = group * TILE + tile * SUBLANES + r
+                for h in halves:
+                    parts = [panel[t][h] for t in tiles[tile:]]
+                    row = row_of(parts[0], r)
+                    if h == half:
+                        row = jnp.where(at_lane, 1.0, row)
+                        parts = [jnp.where(at_lane, 0.0, part) for part in parts]
+                    packed[index : index + 1, h * LANES : (h + 1) * LANES] = (row * scale)[0:1]
+                    for t, part in zip(tiles[tile:], eliminated(parts, row)):
+                        panel[t][h] = part
+                if update is not None:
+                    for i in below[1 + tile * SUBLANES + r :: TILE]:
+                        fresh = lowered(i)
+                        for t in tiles:
+                            for h in halves:
+                                work[place_of(i, t, h)] = fresh[t][h]
+            if tile == 0:
+                columns[1] = [
+                    [c[0] - total_of([v * (row_of(v, s) * recip) for v, recip in taken])]
+                    for s, c in enumerate(columns[1])
+                ]
+            right.append(list(panel[tile]))
+            if not below:
+                continue
+            solved = [[row_of(panel[tile][h], q) for h in halves] for q in range(SUBLANES)]
+            for t in tiles:
+                following[t][half] = cleared(following[t][half], origin, SUBLANES)
+                for h in halves:
+                    following[t][h] = following[t][h] - total_of(
+                        [entries[q][t] * solved[q][h] for q in range(SUBLANES)]
+                    )
+        if below:
+            right[0][half] = cleared(right[0][half], start + SUBLANES, SUBLANES)
+            update = (
+                transposed_product(
+                    bf16_parts(whole(left, half), (0, 0, 0, 1, 1, 2)),
+                    bf16_parts(whole(right, 0), (0, 1, 2, 0, 1, 0)),
+                ),
+                half * LANES,
+                half,
+                start,
+            )
+            panel = following
 
     row = lax.broadcasted_iota(jnp.int32, (size, size), 0)
     column = lax.broadcasted_iota(jnp.int32, (size, size), 1)

time: 74.4 us -> 73.4 us (0.987)
  Pallas kernels: 18.2 us -> 14.7 us
  waiting for transfers between devices: 5.09 us -> 7.52 us
    ppermute x1, waiting for transfers between devices: 4.25 us -> 6.67 us  [body(): lax.ppermute(to_outer, chain, [(i, i + 1) for i in pairs] + [(i + 1, i) f...]
    pallas_call x1, Pallas kernels: 4.32 us -> 2.47 us  [own_rows(): pl.pallas_call(own_rows_kernel, out_shape=jax.ShapeDtypeStruct((STACK, LA...]
    pallas_call x1, Pallas kernels: 8.84 us -> 7.85 us  [factor_and_projection(): pl.pallas_call(factor_kernel, out_shape=(jax.ShapeDtypeStruct((MEMBERS, M...]
  transfers between devices with their start and end apart: 3 -> 3, of which waited for: 2 -> 2; matrix products, arithmetic and copies ran while one was open for 0% -> 0% of each run, Pallas kernels for 9% -> 5%
where the time goes in v3:
time: 73.4 us; the launch traced here: 72.3 us
  blocking collectives  37.9 us (52%)
  Pallas kernels  14.7 us (20%)
  starting transfers between devices  10.7 us (15%)
  waiting for transfers between devices  7.52 us (10%)
    all_to_all x2, blocking collectives, to_all(): return lax.all_to_all(copies, axes, 0, 0)  24.9 us
    all_to_all x1, blocking collectives, summed(): piece = lax.all_to_all(pieces, axes, 0, 0).sum(0)  13 us
    pallas_call x1, Pallas kernels, factor_and_projection(): pl.pallas_call(factor_kernel, out_shape=(jax.ShapeDtypeStruct((MEMBERS, M...  7.85 us
    ppermute x1, waiting for transfers between devices, body(): lax.ppermute(to_outer, chain, [(i, i + 1) for i in pairs] + [(i + 1, i) f...  6.67 us
    ppermute x1, starting transfers between devices, summed(): piece = piece + lax.ppermute(piece, 'c', [(0, 1), (1, 0)])  5.47 us
    ppermute x1, starting transfers between devices, body(): inner = lax.ppermute(to_inner, chain, [(i, i ^ 1) for i in range(count)])  3.32 us
    pallas_call x1, Pallas kernels, own_rows(): pl.pallas_call(own_rows_kernel, out_shape=jax.ShapeDtypeStruct((STACK, LA...  2.47 us
    pallas_call x1, Pallas kernels, parcels(): pl.pallas_call(parcels_kernel, out_shape=(parcel, parcel), in_specs=[SMEM...  1.97 us
  transfers between devices with their start and end apart: 3, of which 2 were waited for; matrix products, arithmetic and copies ran while one was open for 0% of the time, Pallas kernels for 5%

profile of v3, /device:TPU:1, one launch (start us, length us, event | category | flops | bytes accessed | tf_op | source)
XLA Modules:
  0.0 72.3 jit_solution(12518023275942021255)
XLA Ops:
  0.6 0.0 copy-start.1
  0.6 0.6 copy-done.1
  1.3 0.0 copy-start
  1.3 2.0 %parcels.1 = (bf16[2816,128]{1,0:T(8,128)(2,1)S(1)}, bf16[2816,128]{1,0:T(8,128)(2,1)S(1)}) custom-call(s32[1]{0:T(128)} %bitcast.core, s32[4]{0:T(128)S(1)} %bitcast.10, bf16[16384,256]{1,0:T(8,128)(2,1)} %bitcast.14, bf16[8192,128]{1,0:T(8,128)(2,1)} %bitcast.6), custom_call_target="tpu_custom_call" | custom-call | bytes 3145728 | tf_op jit(solution)/shard_map/parcels/pallas_call | solution.py:221
  3.3 3.3 %collective-permute-start = (bf16[2816,128]{1,0:T(8,128)(2,1)S(1)}, bf16[2816,128]{1,0:T(8,128)(2,1)S(1)}, u32[]{:S(2)}, u32[]{:S(2)}) collective-permute-start(bf16[2816,128]{1,0:T(8,128)(2,1)S(1)} %get-tuple-element.7), channel_id=1, source_target_pairs={{0,4},{4,0},{8,12},{12,8},{16,20},{20,16},{24,28},{28,24},{32,36},... | collective-permute-start | bytes 2162696 | tf_op jit(solution)/shard_map/ppermute | solution.py:511
  6.6 1.9 %collective-permute-start.1 = (bf16[2816,128]{1,0:T(8,128)(2,1)S(1)}, bf16[2816,128]{1,0:T(8,128)(2,1)S(1)}, u32[]{:S(2)}, u32[]{:S(2)}) collective-permute-start(bf16[2816,128]{1,0:T(8,128)(2,1)S(1)} %get-tuple-element.10), channel_id=1, source_target_pairs={{4,8},{12,16},{20,24},{28,32},{36,40},{44,48},{52,56},{60,64},{68,... | collective-permute-start | bytes 2162696 | tf_op jit(solution)/shard_map/ppermute | solution.py:508
  8.5 0.0 copy-done
  8.5 2.5 %own_rows.1.before = f32[640,128]{1,0:T(8,128)S(1)} custom-call(s32[4]{0:T(128)S(1)} %bitcast.11, bf16[16384,256]{1,0:T(8,128)(2,1)} %bitcast.15, bf16[8192,128]{1,0:T(8,128)(2,1)S(1)} %bitcast.7), custom_call_target="tpu_custom_call" | custom-call | flops 2415919104 | bytes 10485760 | tf_op jit(solution)/shard_map/own_rows/pallas_call | solution.py:235
  11.0 0.0 collective-permute-done.parcel
  11.0 1.5 %inner_edge.1 = (f32[640,128]{1,0:T(8,128)S(1)}, bf16[5376,256]{1,0:T(8,128)(2,1)S(1)}, bf16[1408,128]{1,0:T(8,128)(2,1)S(1)}) custom-call(s32[1]{0:T(128)} %bitcast.core, s32[4]{0:T(128)S(1)} %bitcast.12, bf16[16384,256]{1,0:T(8,128)(2,1)} %bitcast.16, bf16[8192,128]{1,0:T(8,128)(2,1)S(1)} %bitcast.8, bf16[2816,128]{1,0:T(8,128)(2,1)S(1)} %collective-permute-done.parcel, ...), custom_call_target="tpu_custom_call" | custom-call | flops 134217728 | bytes 4194304 | tf_op jit(solution)/shard_map/inner_edge/pallas_call | solution.py:259
  12.5 6.7 %collective-permute-done.1.parcel = bf16[2816,128]{1,0:T(8,128)(2,1)S(1)} collective-permute-done((bf16[2816,128]{1,0:T(8,128)(2,1)S(1)}, bf16[2816,128]{1,0:T(8,128)(2,1)S(1)}, u32[]{:S(2)}, u32[]{:S(2)}) %collective-permute-start.1) | collective-permute-done | bytes 720928 | tf_op jit(solution)/shard_map/ppermute | solution.py:508
  19.2 1.0 %outer_edge.1 = f32[640,128]{1,0:T(8,128)S(1)} custom-call(s32[1]{0:T(128)} %bitcast.core, s32[4]{0:T(128)S(1)} %bitcast.13, bf16[5376,256]{1,0:T(8,128)(2,1)S(1)} %get-tuple-element.8.outer_near, bf16[1408,128]{1,0:T(8,128)(2,1)S(1)} %get-tuple-element.9.outer_far, bf16[2816,128]{1,0:T(8,128)(2,1)S(1)} %collective-permute-done.1.parcel, ...), custom_call_target="tpu_custom_call" | custom-call | flops 134217728 | bytes 2097152 | tf_op jit(solution)/shard_map/outer_edge/pallas_call | solution.py:282
  20.1 13.0 %all_to_all.15 = f32[16,40,128]{2,1,0:T(8,128)S(1)} all-to-all(f32[16,40,128]{2,1,0:T(8,128)S(1)} %bitcast.9), channel_id=1, replica_groups=mesh['y'=4,'z'=8,'c'=2,'g'=4] {'y','g'}, dimensions={0} | all-to-all | bytes 655360 | tf_op jit(solution)/shard_map/all_to_all | solution.py:493
  33.2 5.5 %collective-permute-start.2 = (f32[40,128]{1,0:T(8,128)S(1)}, f32[40,128]{1,0:T(8,128)S(1)}, u32[]{:S(2)}, u32[]{:S(2)}) collective-permute-start(f32[40,128]{1,0:T(8,128)S(1)} %reduce_sum.18), channel_id=1, source_target_pairs={{0,4},{4,0},{1,5},{5,1},{2,6},{6,2},{3,7},{7,3},{8,12},{12,8},{9,1... | collective-permute-start | bytes 61448 | tf_op jit(solution)/shard_map/ppermute | solution.py:494
  38.7 0.8 %collective-permute-done.2 = f32[40,128]{1,0:T(8,128)S(1)} collective-permute-done((f32[40,128]{1,0:T(8,128)S(1)}, f32[40,128]{1,0:T(8,128)S(1)}, u32[]{:S(2)}, u32[]{:S(2)}) %collective-permute-start.2) | collective-permute-done | bytes 20512 | tf_op jit(solution)/shard_map/ppermute | solution.py:494
  39.5 13.7 %all_to_all.16 = f32[8,40,128]{2,1,0:T(8,128)S(1)} all-to-all(f32[8,40,128]{2,1,0:T(8,128)S(1)} %broadcast_in_dim.4), channel_id=1, replica_groups=mesh['y'=4,'z'=8,'c'=2,'g'=4] {'z'}, dimensions={0} | all-to-all | bytes 327680 | tf_op jit(solution)/shard_map/all_to_all | solution.py:486
  53.3 11.2 %all_to_all.17 = f32[16,40,128]{2,1,0:T(8,128)} all-to-all(f32[16,40,128]{2,1,0:T(8,128)S(1)} %broadcast_in_dim.5), channel_id=1, replica_groups=mesh['y'=4,'z'=8,'c'=2,'g'=4] {'y','g'}, dimensions={0} | all-to-all | bytes 655360 | tf_op jit(solution)/shard_map/all_to_all | solution.py:486
  64.5 7.8 %factor_and_projection.1 = (f32[256,256]{1,0:T(8,128)}, f32[128,256]{1,0:T(8,128)}) custom-call(f32[640,128]{1,0:T(8,128)} %bitcast.17), custom_call_target="tpu_custom_call" | custom-call | tf_op jit(solution)/shard_map/factor_and_projection/pallas_call | solution.py:466
  (5 shorter events, 0.1 us)
Async XLA Ops:
  0.6 0.7 copy-start.1
  1.3 7.2 %copy-start = (bf16[1,8192,128]{2,1,0:T(8,128)(2,1)S(1)}, bf16[1,8192,128]{2,1,0:T(8,128)(2,1)}, u32[]{:S(2)}) copy-start(bf16[1,8192,128]{2,1,0:T(8,128)(2,1)} %param.5) | copy-start | bytes 6291460
  3.3 7.7 %collective-permute-start = (bf16[2816,128]{1,0:T(8,128)(2,1)S(1)}, bf16[2816,128]{1,0:T(8,128)(2,1)S(1)}, u32[]{:S(2)}, u32[]{:S(2)}) collective-permute-start(bf16[2816,128]{1,0:T(8,128)(2,1)S(1)} %get-tuple-element.7), channel_id=1, source_target_pairs={{0,4},{4,0},{8,12},{12,8},{16,20},{20,16},{24,28},{28,24},{32,36},... | collective-permute-start | bytes 2162696 | tf_op jit(solution)/shard_map/ppermute | solution.py:511
  6.6 12.6 %collective-permute-start.1 = (bf16[2816,128]{1,0:T(8,128)(2,1)S(1)}, bf16[2816,128]{1,0:T(8,128)(2,1)S(1)}, u32[]{:S(2)}, u32[]{:S(2)}) collective-permute-start(bf16[2816,128]{1,0:T(8,128)(2,1)S(1)} %get-tuple-element.10), channel_id=1, source_target_pairs={{4,8},{12,16},{20,24},{28,32},{36,40},{44,48},{52,56},{60,64},{68,... | collective-permute-start | bytes 2162696 | tf_op jit(solution)/shard_map/ppermute | solution.py:508
  33.2 6.3 %collective-permute-start.2 = (f32[40,128]{1,0:T(8,128)S(1)}, f32[40,128]{1,0:T(8,128)S(1)}, u32[]{:S(2)}, u32[]{:S(2)}) collective-permute-start(f32[40,128]{1,0:T(8,128)S(1)} %reduce_sum.18), channel_id=1, source_target_pairs={{0,4},{4,0},{1,5},{5,1},{2,6},{6,2},{3,7},{7,3},{8,12},{12,8},{9,1... | collective-permute-start | bytes 61448 | tf_op jit(solution)/shard_map/ppermute | solution.py:494

commit v4 on v3

--- a/solution.py
+++ b/solution.py
@@ -12,7 +12,7 @@
 MEMBERS = 256
 MODES = 128
 BLOCKS = 64
-CHUNK = 16
+CHUNK = 32
 CHUNK_ROWS = CHUNK * BLOCK
 SUBLANES = 8
 TILE = 16
@@ -22,6 +22,7 @@
 NEAR_ROWS = NEAR * BLOCK
 FAR_ROWS = FAR * BLOCK
 PARCEL = 2 * FAR_ROWS
+OUTER_PARCEL = PARCEL + 16
 VMEM_BYTES = 51 * 1024 * 1024
 EDGE_VMEM_BYTES = 45 * 1024 * 1024
 
@@ -217,10 +218,12 @@
 
 
 def parcels(core, moves, panel, modes):
-    parcel = jax.ShapeDtypeStruct((PARCEL, LANES), modes.dtype)
     return pl.pallas_call(
         parcels_kernel,
-        out_shape=(parcel, parcel),
+        out_shape=(
+            jax.ShapeDtypeStruct((PARCEL, LANES), modes.dtype),
+            jax.ShapeDtypeStruct((OUTER_PARCEL, LANES), modes.dtype),
+        ),
         in_specs=[SMEM, SMEM, HBM, HBM],
         out_specs=(VMEM, VMEM),
         scratch_shapes=[pltpu.SemaphoreType.DMA((2, 2))],
@@ -272,7 +275,7 @@
         ],
         compiler_params=pltpu.CompilerParams(vmem_limit_bytes=EDGE_VMEM_BYTES),
         cost_estimate=pl.CostEstimate(
-            flops=2 * 2048 * 128 * 256, bytes_accessed=4 * 1024 * 1024, transcendentals=0
+            flops=0, bytes_accessed=1024, transcendentals=0
         ),
         name="inner_edge",
     )(core, moves, panel, modes, parcel, before)
@@ -286,7 +289,7 @@
         out_specs=VMEM,
         compiler_params=pltpu.CompilerParams(vmem_limit_bytes=EDGE_VMEM_BYTES),
         cost_estimate=pl.CostEstimate(
-            flops=2 * 2048 * 128 * 256, bytes_accessed=2 * 1024 * 1024, transcendentals=0
+            flops=0, bytes_accessed=1024, transcendentals=0
         ),
         name="outer_edge",
     )(core, moves, near, far, parcel, before)

time: 73.4 us -> 73.3 us (level)
  waiting for transfers between devices: 7.52 us -> 1.1 us
  blocking collectives: 37.9 us -> 43.8 us
  Pallas kernels: 14.7 us -> 19.4 us
  starting transfers between devices: 10.7 us -> 6.52 us
    ppermute x1, waiting for transfers between devices: 6.67 us -> 0.25 us  [body(): lax.ppermute(to_outer, chain, [(i, i + 1) for i in pairs] + [(i + 1, i) f...]
    all_to_all x1, blocking collectives: 13 us -> 19 us  [summed(): piece = lax.all_to_all(pieces, axes, 0, 0).sum(0)]
    ppermute x1, starting transfers between devices: 5.47 us -> 1.49 us  [summed(): piece = piece + lax.ppermute(piece, 'c', [(0, 1), (1, 0)])]
    pallas_call x1, Pallas kernels: 2.47 us -> 6.26 us  [own_rows(): pl.pallas_call(own_rows_kernel, out_shape=jax.ShapeDtypeStruct((STACK, LA...]
    ppermute x1, starting transfers between devices: 3.32 us -> 0.09 us  [body(): inner = lax.ppermute(to_inner, chain, [(i, i ^ 1) for i in range(count)])]
    ppermute x1, starting transfers between devices: 1.91 us -> 4.93 us  [body(): lax.ppermute(to_outer, chain, [(i, i + 1) for i in pairs] + [(i + 1, i) f...]
    pallas_call x1, Pallas kernels: 1.5 us -> 2.35 us  [inner_edge(): pl.pallas_call(inner_edge_kernel, out_shape=(jax.ShapeDtypeStruct((STACK,...]
  transfers between devices with their start and end apart: 3 -> 3, of which waited for: 2 -> 2; matrix products, arithmetic and copies ran while one was open for 0% -> 0% of each run, Pallas kernels for 5% -> 12%
where the time goes in v4:
time: 73.3 us; the launch traced here: 72.2 us
  blocking collectives  43.8 us (60%)
  Pallas kernels  19.4 us (26%)
  starting transfers between devices  6.52 us (9%)
  waiting for transfers between devices  1.1 us (2%)
    all_to_all x2, blocking collectives, to_all(): return lax.all_to_all(copies, axes, 0, 0)  24.8 us
    all_to_all x1, blocking collectives, summed(): piece = lax.all_to_all(pieces, axes, 0, 0).sum(0)  19 us
    pallas_call x1, Pallas kernels, factor_and_projection(): pl.pallas_call(factor_kernel, out_shape=(jax.ShapeDtypeStruct((MEMBERS, M...  7.85 us
    pallas_call x1, Pallas kernels, own_rows(): pl.pallas_call(own_rows_kernel, out_shape=jax.ShapeDtypeStruct((STACK, LA...  6.26 us
    ppermute x1, starting transfers between devices, body(): lax.ppermute(to_outer, chain, [(i, i + 1) for i in pairs] + [(i + 1, i) f...  4.93 us
    pallas_call x1, Pallas kernels, inner_edge(): pl.pallas_call(inner_edge_kernel, out_shape=(jax.ShapeDtypeStruct((STACK,...  2.35 us
    pallas_call x1, Pallas kernels, parcels(): pl.pallas_call(parcels_kernel, out_shape=(jax.ShapeDtypeStruct((PARCEL, L...  1.97 us
    ppermute x1, starting transfers between devices, summed(): piece = piece + lax.ppermute(piece, 'c', [(0, 1), (1, 0)])  1.49 us
  transfers between devices with their start and end apart: 3, of which 2 were waited for; matrix products, arithmetic and copies ran while one was open for 0% of the time, Pallas kernels for 12%

profile of v4, /device:TPU:1, one launch (start us, length us, event | category | flops | bytes accessed | tf_op | source)
XLA Modules:
  0.0 72.2 jit_solution(10844231939660787524)
XLA Ops:
  0.6 0.0 copy-start.1
  0.6 0.6 copy-done.1
  1.3 0.0 copy-start
  1.3 2.0 %parcels.1 = (bf16[2816,128]{1,0:T(8,128)(2,1)S(1)}, bf16[2832,128]{1,0:T(8,128)(2,1)S(1)}) custom-call(s32[1]{0:T(128)} %bitcast.core, s32[4]{0:T(128)S(1)} %bitcast.10, bf16[16384,256]{1,0:T(8,128)(2,1)} %bitcast.14, bf16[8192,128]{1,0:T(8,128)(2,1)} %bitcast.6), custom_call_target="tpu_custom_call" | custom-call | bytes 3145728 | tf_op jit(solution)/shard_map/parcels/pallas_call | solution.py:221
  3.3 4.9 %collective-permute-start.1 = (bf16[2832,128]{1,0:T(8,128)(2,1)S(1)}, bf16[2832,128]{1,0:T(8,128)(2,1)S(1)}, u32[]{:S(2)}, u32[]{:S(2)}) collective-permute-start(bf16[2832,128]{1,0:T(8,128)(2,1)S(1)} %get-tuple-element.10), channel_id=1, source_target_pairs={{4,8},{12,16},{20,24},{28,32},{36,40},{44,48},{52,56},{60,64},{68,... | collective-permute-start | bytes 2174984 | tf_op jit(solution)/shard_map/ppermute | solution.py:511
  8.2 0.1 collective-permute-start
  8.3 0.0 copy-done
  8.3 6.3 %own_rows.1.before = f32[640,128]{1,0:T(8,128)S(1)} custom-call(s32[4]{0:T(128)S(1)} %bitcast.11, bf16[16384,256]{1,0:T(8,128)(2,1)} %bitcast.15, bf16[8192,128]{1,0:T(8,128)(2,1)S(1)} %bitcast.7), custom_call_target="tpu_custom_call" | custom-call | flops 2415919104 | bytes 10485760 | tf_op jit(solution)/shard_map/own_rows/pallas_call | solution.py:238
  14.6 0.0 collective-permute-done.parcel
  14.6 2.3 %inner_edge.1 = (f32[640,128]{1,0:T(8,128)S(1)}, bf16[5376,256]{1,0:T(8,128)(2,1)S(1)}, bf16[1408,128]{1,0:T(8,128)(2,1)S(1)}) custom-call(s32[1]{0:T(128)} %bitcast.core, s32[4]{0:T(128)S(1)} %bitcast.12, bf16[16384,256]{1,0:T(8,128)(2,1)} %bitcast.16, bf16[8192,128]{1,0:T(8,128)(2,1)S(1)} %bitcast.8, bf16[2816,128]{1,0:T(8,128)(2,1)S(1)} %collective-permute-done.parcel, ...), custom_call_target="tpu_custom_call" | custom-call | bytes 1024 | tf_op jit(solution)/shard_map/inner_edge/pallas_call | solution.py:262
  17.0 0.3 collective-permute-done.1.parcel
  17.2 1.0 %outer_edge.1 = f32[640,128]{1,0:T(8,128)S(1)} custom-call(s32[1]{0:T(128)} %bitcast.core, s32[4]{0:T(128)S(1)} %bitcast.13, bf16[5376,256]{1,0:T(8,128)(2,1)S(1)} %get-tuple-element.8.outer_near, bf16[1408,128]{1,0:T(8,128)(2,1)S(1)} %get-tuple-element.9.outer_far, bf16[2832,128]{1,0:T(8,128)(2,1)S(1)} %collective-permute-done.1.parcel, ...), custom_call_target="tpu_custom_call" | custom-call | bytes 1024 | tf_op jit(solution)/shard_map/outer_edge/pallas_call | solution.py:285
  18.2 19.0 %all_to_all.15 = f32[16,40,128]{2,1,0:T(8,128)S(1)} all-to-all(f32[16,40,128]{2,1,0:T(8,128)S(1)} %bitcast.9), channel_id=1, replica_groups=mesh['y'=4,'z'=8,'c'=2,'g'=4] {'y','g'}, dimensions={0} | all-to-all | bytes 655360 | tf_op jit(solution)/shard_map/all_to_all | solution.py:496
  37.2 1.5 %collective-permute-start.2 = (f32[40,128]{1,0:T(8,128)S(1)}, f32[40,128]{1,0:T(8,128)S(1)}, u32[]{:S(2)}, u32[]{:S(2)}) collective-permute-start(f32[40,128]{1,0:T(8,128)S(1)} %reduce_sum.18), channel_id=1, source_target_pairs={{0,4},{4,0},{1,5},{5,1},{2,6},{6,2},{3,7},{7,3},{8,12},{12,8},{9,1... | collective-permute-start | bytes 61448 | tf_op jit(solution)/shard_map/ppermute | solution.py:497
  38.7 0.8 %collective-permute-done.2 = f32[40,128]{1,0:T(8,128)S(1)} collective-permute-done((f32[40,128]{1,0:T(8,128)S(1)}, f32[40,128]{1,0:T(8,128)S(1)}, u32[]{:S(2)}, u32[]{:S(2)}) %collective-permute-start.2) | collective-permute-done | bytes 20512 | tf_op jit(solution)/shard_map/ppermute | solution.py:497
  39.6 13.5 %all_to_all.16 = f32[8,40,128]{2,1,0:T(8,128)S(1)} all-to-all(f32[8,40,128]{2,1,0:T(8,128)S(1)} %broadcast_in_dim.4), channel_id=1, replica_groups=mesh['y'=4,'z'=8,'c'=2,'g'=4] {'z'}, dimensions={0} | all-to-all | bytes 327680 | tf_op jit(solution)/shard_map/all_to_all | solution.py:489
  53.2 11.2 %all_to_all.17 = f32[16,40,128]{2,1,0:T(8,128)} all-to-all(f32[16,40,128]{2,1,0:T(8,128)S(1)} %broadcast_in_dim.5), channel_id=1, replica_groups=mesh['y'=4,'z'=8,'c'=2,'g'=4] {'y','g'}, dimensions={0} | all-to-all | bytes 655360 | tf_op jit(solution)/shard_map/all_to_all | solution.py:489
  64.4 7.9 %factor_and_projection.1 = (f32[256,256]{1,0:T(8,128)}, f32[128,256]{1,0:T(8,128)}) custom-call(f32[640,128]{1,0:T(8,128)} %bitcast.17), custom_call_target="tpu_custom_call" | custom-call | tf_op jit(solution)/shard_map/factor_and_projection/pallas_call | solution.py:469
  (5 shorter events, 0.1 us)
Async XLA Ops:
  0.6 0.7 copy-start.1
  1.3 7.0 %copy-start = (bf16[1,8192,128]{2,1,0:T(8,128)(2,1)S(1)}, bf16[1,8192,128]{2,1,0:T(8,128)(2,1)}, u32[]{:S(2)}) copy-start(bf16[1,8192,128]{2,1,0:T(8,128)(2,1)} %param.5) | copy-start | bytes 6291460
  3.3 13.9 %collective-permute-start.1 = (bf16[2832,128]{1,0:T(8,128)(2,1)S(1)}, bf16[2832,128]{1,0:T(8,128)(2,1)S(1)}, u32[]{:S(2)}, u32[]{:S(2)}) collective-permute-start(bf16[2832,128]{1,0:T(8,128)(2,1)S(1)} %get-tuple-element.10), channel_id=1, source_target_pairs={{4,8},{12,16},{20,24},{28,32},{36,40},{44,48},{52,56},{60,64},{68,... | collective-permute-start | bytes 2174984 | tf_op jit(solution)/shard_map/ppermute | solution.py:511
  8.2 6.4 %collective-permute-start = (bf16[2816,128]{1,0:T(8,128)(2,1)S(1)}, bf16[2816,128]{1,0:T(8,128)(2,1)S(1)}, u32[]{:S(2)}, u32[]{:S(2)}) collective-permute-start(bf16[2816,128]{1,0:T(8,128)(2,1)S(1)} %get-tuple-element.7), channel_id=1, source_target_pairs={{0,4},{4,0},{8,12},{12,8},{16,20},{20,16},{24,28},{28,24},{32,36},... | collective-permute-start | bytes 2162696 | tf_op jit(solution)/shard_map/ppermute | solution.py:514
  37.2 2.3 %collective-permute-start.2 = (f32[40,128]{1,0:T(8,128)S(1)}, f32[40,128]{1,0:T(8,128)S(1)}, u32[]{:S(2)}, u32[]{:S(2)}) collective-permute-start(f32[40,128]{1,0:T(8,128)S(1)} %reduce_sum.18), channel_id=1, source_target_pairs={{0,4},{4,0},{1,5},{5,1},{2,6},{6,2},{3,7},{7,3},{8,12},{12,8},{9,1... | collective-permute-start | bytes 61448 | tf_op jit(solution)/shard_map/ppermute | solution.py:497

commit v5 on v4

--- a/solution.py
+++ b/solution.py
@@ -490,7 +490,7 @@
 
 
 def summed(stack):
-    axes = ("y", "g")
+    axes = ("g", "y")
     count = lax.axis_size(axes)
     pieces = stack.reshape(count, stack.shape[0] // count, LANES)
     piece = lax.all_to_all(pieces, axes, 0, 0).sum(0)

time: 73.3 us -> 72.9 us (level)
  Pallas kernels: 19.4 us -> 17 us
  waiting for transfers between devices: 1.1 us -> 3.15 us
  blocking collectives: 43.8 us -> 42.8 us
  starting transfers between devices: 6.52 us -> 7.38 us
    ppermute x1, waiting for transfers between devices: 0.25 us -> 2.3 us  [body(): lax.ppermute(to_outer, chain, [(i, i + 1) for i in pairs] + [(i + 1, i) f...]
    pallas_call x1, Pallas kernels: 6.26 us -> 4.22 us  [own_rows(): pl.pallas_call(own_rows_kernel, out_shape=jax.ShapeDtypeStruct((STACK, LA...]
    all_to_all x1, blocking collectives: 19 us -> 17.9 us  [summed(): piece = lax.all_to_all(pieces, axes, 0, 0).sum(0)]
    ppermute x1, starting transfers between devices: 1.49 us -> 2.35 us  [summed(): piece = piece + lax.ppermute(piece, 'c', [(0, 1), (1, 0)])]
  transfers between devices with their start and end apart: 3 -> 3, of which waited for: 2 -> 2; matrix products, arithmetic and copies ran while one was open for 0% -> 0% of each run, Pallas kernels for 12% -> 9%
where the time goes in v5:
time: 72.9 us; the launch traced here: 71.8 us
  blocking collectives  42.8 us (59%)
  Pallas kernels  17 us (23%)
  starting transfers between devices  7.38 us (10%)
  waiting for transfers between devices  3.15 us (4%)
  between operations  0.73 us (1%)
    all_to_all x2, blocking collectives, to_all(): return lax.all_to_all(copies, axes, 0, 0)  24.9 us
    all_to_all x1, blocking collectives, summed(): piece = lax.all_to_all(pieces, axes, 0, 0).sum(0)  17.9 us
    pallas_call x1, Pallas kernels, factor_and_projection(): pl.pallas_call(factor_kernel, out_shape=(jax.ShapeDtypeStruct((MEMBERS, M...  7.85 us
    ppermute x1, starting transfers between devices, body(): lax.ppermute(to_outer, chain, [(i, i + 1) for i in pairs] + [(i + 1, i) f...  4.94 us
    pallas_call x1, Pallas kernels, own_rows(): pl.pallas_call(own_rows_kernel, out_shape=jax.ShapeDtypeStruct((STACK, LA...  4.22 us
    ppermute x1, starting transfers between devices, summed(): piece = piece + lax.ppermute(piece, 'c', [(0, 1), (1, 0)])  2.35 us
    pallas_call x1, Pallas kernels, inner_edge(): pl.pallas_call(inner_edge_kernel, out_shape=(jax.ShapeDtypeStruct((STACK,...  2.34 us
    ppermute x1, waiting for transfers between devices, body(): lax.ppermute(to_outer, chain, [(i, i + 1) for i in pairs] + [(i + 1, i) f...  2.3 us
  transfers between devices with their start and end apart: 3, of which 2 were waited for; matrix products, arithmetic and copies ran while one was open for 0% of the time, Pallas kernels for 9%

profile of v5, /device:TPU:1, one launch (start us, length us, event | category | flops | bytes accessed | tf_op | source)
XLA Modules:
  0.0 71.8 jit_solution(6727956305528202025)
XLA Ops:
  0.6 0.0 copy-start.1
  0.6 0.6 copy-done.1
  1.3 0.0 copy-start
  1.3 2.0 %parcels.1 = (bf16[2816,128]{1,0:T(8,128)(2,1)S(1)}, bf16[2832,128]{1,0:T(8,128)(2,1)S(1)}) custom-call(s32[1]{0:T(128)} %bitcast.core, s32[4]{0:T(128)S(1)} %bitcast.10, bf16[16384,256]{1,0:T(8,128)(2,1)} %bitcast.14, bf16[8192,128]{1,0:T(8,128)(2,1)} %bitcast.6), custom_call_target="tpu_custom_call" | custom-call | bytes 3145728 | tf_op jit(solution)/shard_map/parcels/pallas_call | solution.py:221
  3.3 4.9 %collective-permute-start.1 = (bf16[2832,128]{1,0:T(8,128)(2,1)S(1)}, bf16[2832,128]{1,0:T(8,128)(2,1)S(1)}, u32[]{:S(2)}, u32[]{:S(2)}) collective-permute-start(bf16[2832,128]{1,0:T(8,128)(2,1)S(1)} %get-tuple-element.10), channel_id=1, source_target_pairs={{4,8},{12,16},{20,24},{28,32},{36,40},{44,48},{52,56},{60,64},{68,... | collective-permute-start | bytes 2174984 | tf_op jit(solution)/shard_map/ppermute | solution.py:511
  8.2 0.1 collective-permute-start
  8.3 0.0 copy-done
  8.3 4.2 %own_rows.1.before = f32[640,128]{1,0:T(8,128)S(1)} custom-call(s32[4]{0:T(128)S(1)} %bitcast.11, bf16[16384,256]{1,0:T(8,128)(2,1)} %bitcast.15, bf16[8192,128]{1,0:T(8,128)(2,1)S(1)} %bitcast.7), custom_call_target="tpu_custom_call" | custom-call | flops 2415919104 | bytes 10485760 | tf_op jit(solution)/shard_map/own_rows/pallas_call | solution.py:238
  12.6 0.0 collective-permute-done.parcel
  12.6 2.3 %inner_edge.1 = (f32[640,128]{1,0:T(8,128)S(1)}, bf16[5376,256]{1,0:T(8,128)(2,1)S(1)}, bf16[1408,128]{1,0:T(8,128)(2,1)S(1)}) custom-call(s32[1]{0:T(128)} %bitcast.core, s32[4]{0:T(128)S(1)} %bitcast.12, bf16[16384,256]{1,0:T(8,128)(2,1)} %bitcast.16, bf16[8192,128]{1,0:T(8,128)(2,1)S(1)} %bitcast.8, bf16[2816,128]{1,0:T(8,128)(2,1)S(1)} %collective-permute-done.parcel, ...), custom_call_target="tpu_custom_call" | custom-call | bytes 1024 | tf_op jit(solution)/shard_map/inner_edge/pallas_call | solution.py:262
  14.9 2.3 %collective-permute-done.1.parcel = bf16[2832,128]{1,0:T(8,128)(2,1)S(1)} collective-permute-done((bf16[2832,128]{1,0:T(8,128)(2,1)S(1)}, bf16[2832,128]{1,0:T(8,128)(2,1)S(1)}, u32[]{:S(2)}, u32[]{:S(2)}) %collective-permute-start.1) | collective-permute-done | bytes 725024 | tf_op jit(solution)/shard_map/ppermute | solution.py:511
  17.2 0.6 outer_edge.1
  17.8 17.9 %all_to_all.15 = f32[16,40,128]{2,1,0:T(8,128)S(1)} all-to-all(f32[16,40,128]{2,1,0:T(8,128)S(1)} %bitcast.9), channel_id=1, replica_groups=mesh['y'=4,'z'=8,'c'=2,'g'=4] {'g','y'}, dimensions={0} | all-to-all | bytes 655360 | tf_op jit(solution)/shard_map/all_to_all | solution.py:496
  35.8 2.4 %collective-permute-start.2 = (f32[40,128]{1,0:T(8,128)S(1)}, f32[40,128]{1,0:T(8,128)S(1)}, u32[]{:S(2)}, u32[]{:S(2)}) collective-permute-start(f32[40,128]{1,0:T(8,128)S(1)} %reduce_sum.18), channel_id=1, source_target_pairs={{0,4},{4,0},{1,5},{5,1},{2,6},{6,2},{3,7},{7,3},{8,12},{12,8},{9,1... | collective-permute-start | bytes 61448 | tf_op jit(solution)/shard_map/ppermute | solution.py:497
  38.1 0.8 %collective-permute-done.2 = f32[40,128]{1,0:T(8,128)S(1)} collective-permute-done((f32[40,128]{1,0:T(8,128)S(1)}, f32[40,128]{1,0:T(8,128)S(1)}, u32[]{:S(2)}, u32[]{:S(2)}) %collective-permute-start.2) | collective-permute-done | bytes 20512 | tf_op jit(solution)/shard_map/ppermute | solution.py:497
  39.0 13.9 %all_to_all.16 = f32[8,40,128]{2,1,0:T(8,128)S(1)} all-to-all(f32[8,40,128]{2,1,0:T(8,128)S(1)} %broadcast_in_dim.4), channel_id=1, replica_groups=mesh['y'=4,'z'=8,'c'=2,'g'=4] {'z'}, dimensions={0} | all-to-all | bytes 327680 | tf_op jit(solution)/shard_map/all_to_all | solution.py:489
  52.9 11.0 %all_to_all.17 = f32[16,40,128]{2,1,0:T(8,128)} all-to-all(f32[16,40,128]{2,1,0:T(8,128)S(1)} %broadcast_in_dim.5), channel_id=1, replica_groups=mesh['y'=4,'z'=8,'c'=2,'g'=4] {'g','y'}, dimensions={0} | all-to-all | bytes 655360 | tf_op jit(solution)/shard_map/all_to_all | solution.py:489
  63.9 7.8 %factor_and_projection.1 = (f32[256,256]{1,0:T(8,128)}, f32[128,256]{1,0:T(8,128)}) custom-call(f32[640,128]{1,0:T(8,128)} %bitcast.17), custom_call_target="tpu_custom_call" | custom-call | tf_op jit(solution)/shard_map/factor_and_projection/pallas_call | solution.py:469
  (5 shorter events, 0.1 us)
Async XLA Ops:
  0.6 0.7 copy-start.1
  1.3 7.0 %copy-start = (bf16[1,8192,128]{2,1,0:T(8,128)(2,1)S(1)}, bf16[1,8192,128]{2,1,0:T(8,128)(2,1)}, u32[]{:S(2)}) copy-start(bf16[1,8192,128]{2,1,0:T(8,128)(2,1)} %param.5) | copy-start | bytes 6291460
  3.3 13.9 %collective-permute-start.1 = (bf16[2832,128]{1,0:T(8,128)(2,1)S(1)}, bf16[2832,128]{1,0:T(8,128)(2,1)S(1)}, u32[]{:S(2)}, u32[]{:S(2)}) collective-permute-start(bf16[2832,128]{1,0:T(8,128)(2,1)S(1)} %get-tuple-element.10), channel_id=1, source_target_pairs={{4,8},{12,16},{20,24},{28,32},{36,40},{44,48},{52,56},{60,64},{68,... | collective-permute-start | bytes 2174984 | tf_op jit(solution)/shard_map/ppermute | solution.py:511
  8.2 4.3 %collective-permute-start = (bf16[2816,128]{1,0:T(8,128)(2,1)S(1)}, bf16[2816,128]{1,0:T(8,128)(2,1)S(1)}, u32[]{:S(2)}, u32[]{:S(2)}) collective-permute-start(bf16[2816,128]{1,0:T(8,128)(2,1)S(1)} %get-tuple-element.7), channel_id=1, source_target_pairs={{0,4},{4,0},{8,12},{12,8},{16,20},{20,16},{24,28},{28,24},{32,36},... | collective-permute-start | bytes 2162696 | tf_op jit(solution)/shard_map/ppermute | solution.py:514
  35.8 3.2 %collective-permute-start.2 = (f32[40,128]{1,0:T(8,128)S(1)}, f32[40,128]{1,0:T(8,128)S(1)}, u32[]{:S(2)}, u32[]{:S(2)}) collective-permute-start(f32[40,128]{1,0:T(8,128)S(1)} %reduce_sum.18), channel_id=1, source_target_pairs={{0,4},{4,0},{1,5},{5,1},{2,6},{6,2},{3,7},{7,3},{8,12},{12,8},{9,1... | collective-permute-start | bytes 61448 | tf_op jit(solution)/shard_map/ppermute | solution.py:497
